TPU v7x, 128 devices: a whole 4x4x4 slice. The times are simulated.
128 devices in a mesh: wide: 64 (over y, z, x_lo, core), narrow: 2 (over x_hi).
Axes of the slice: x: 4 (x_hi: 2, x_lo: 2; x = x_hi * 2 + x_lo), y: 4, z: 4, core: 2. Of those that a mesh axis runs over, the one named last changes fastest.
Arguments:
- moments: float32 [8192, 1024], P(('wide', 'narrow')), may hold values from -6 to 6
- up_0: bfloat16 [8192, 4096], P(('wide', 'narrow')), may hold values from -0.5 to 0.5
- up_1: bfloat16 [2048, 4096], P(('wide', 'narrow')), may hold values from -0.5 to 0.5
- up_2: bfloat16 [512, 4096], P(('wide', 'narrow')), may hold values from -0.5 to 0.5
- up_3: bfloat16 [128, 4096], P(('wide', 'narrow')), may hold values from -0.5 to 0.5
- couple_0: bfloat16 [229376, 4096], P(('wide', 'narrow')), may hold values from -0.125 to 0.125
- couple_1: bfloat16 [57344, 4096], P(('wide', 'narrow')), may hold values from -0.125 to 0.125
- couple_2: bfloat16 [14336, 4096], P(('wide', 'narrow')), may hold values from -0.125 to 0.125
- couple_3: bfloat16 [3584, 4096], P(('wide', 'narrow')), may hold values from -0.125 to 0.125
- couple_4: bfloat16 [896, 4096], P(('wide', 'narrow')), may hold values from -0.125 to 0.125
- sources_0: int32 [229376], P(('wide', 'narrow')), may hold values from 0 to 8191, as said below
- sources_1: int32 [57344], P(('wide', 'narrow')), may hold values from 0 to 2047, as said below
- sources_2: int32 [14336], P(('wide', 'narrow')), may hold values from 0 to 511, as said below
- sources_3: int32 [3584], P(('wide', 'narrow')), may hold values from 0 to 127, as said below
- sources_4: int32 [896], P(('wide', 'narrow')), may hold values from 0 to 31, as said below
- counts_0: int32 [8192], P(('wide', 'narrow')), may hold values from 14 to 28, as said below
- counts_1: int32 [2048], P(('wide', 'narrow')), may hold values from 14 to 28, as said below
- counts_2: int32 [512], P(('wide', 'narrow')), may hold values from 14 to 28, as said below
- counts_3: int32 [128], P(('wide', 'narrow')), may hold values from 14 to 28, as said below
- counts_4: int32 [32], replicated, may hold values from 14 to 28, as said below
Outputs:
- far_local: float32 [8192, 1024], P(('wide', 'narrow'))
Inputs may be any that keep to these rules, and one draw needn't show every extreme that they name: `sources_0`: slot s belongs to box floor(s / 28). With the level's boxes split evenly over all devices in tree order, every source lies in a box of a device at most 4 devices away from the device of the slot's box; that distance 4 is reached on both sides. `sources_1`: as for sources_0, at level 1. `sources_2`: as for sources_0, at level 2. `sources_3`: as for sources_0, at level 3. `sources_4`: slot s belongs to box floor(s / 28); sources may be any box of level 4. Only the first counts_0[t] slots of box t are valid. Only the first counts_1[t] slots of box t are valid. Only the first counts_2[t] slots of box t are valid. Only the first counts_3[t] slots of box t are valid. Only the first counts_4[t] slots of box t are valid.
All inputs are finite; a program needn't handle non-finite values.
Results may differ from a plain program's by a relative error of at most 0.014.
Values may be sent and summed in bfloat16 or wider, within the bound.
A program may use at most 192 MiB of HBM per device.

v0:
```python
import jax
import jax.numpy as jnp
from jax import lax
from jax.sharding import PartitionSpec as P

RANK = 64
RHS = 16
LIST = 28
REACH = 4


def passed_along(array, axis, by):
    devices = lax.axis_size(axis)
    pairs = [(i, i + by) for i in range(devices) if 0 <= i + by < devices]
    return lax.ppermute(array, axis, pairs)


def partner(block, axis, distance):
    count = lax.axis_size(axis)
    route = []
    for low in range(count):
        high = low | 1 << distance
        if high != low and high < count:
            route += [(low, high), (high, low)]
    return lax.ppermute(block, axis, route)


def lift_terms(moment_rows, transfer):
    boxes = moment_rows.shape[0]
    product = jnp.einsum(
        "crk,ckq->crq",
        moment_rows.reshape(boxes, RHS, RANK),
        transfer.reshape(boxes, RANK, RANK),
        preferred_element_type=jnp.float32,
    )
    return product.reshape(boxes, RHS * RANK)


def lower_terms(far_rows, parent_field, transfer):
    boxes = transfer.shape[0]
    repeats = boxes // parent_field.shape[0]
    parent_rows = jnp.repeat(parent_field.astype(jnp.bfloat16), repeats, axis=0)
    product = jnp.einsum(
        "crq,ckq->crk",
        parent_rows.reshape(boxes, RHS, RANK),
        transfer.reshape(boxes, RANK, RANK),
        preferred_element_type=jnp.float32,
    )
    return far_rows + product.reshape(boxes, RHS * RANK)


def window_rows(coefficients, position):
    pieces = []
    for offset in range(-REACH, REACH + 1):
        if offset == 0:
            pieces.append(coefficients)
        else:
            pieces.append(passed_along(coefficients, ("wide", "narrow"), -offset))
    first_device = position - REACH
    return (jnp.concatenate(pieces, axis=0), first_device)


def far_split(gathered, first_device, per_device, couple, sources, counts):
    local_index = sources - first_device * per_device
    picked = jnp.take(gathered, local_index, axis=0)
    slot_index = jnp.arange(sources.shape[0], dtype=jnp.int32)
    valid = slot_index % LIST < jnp.repeat(counts, LIST)
    picked = jnp.where(valid[:, None], picked, jnp.zeros_like(picked))
    result = jnp.einsum(
        "tjrk,tjkq->trq",
        picked.reshape(per_device, LIST, RHS, RANK),
        couple.reshape(per_device, LIST, RANK, RANK),
        preferred_element_type=jnp.float32,
    )
    return result.reshape(per_device, RHS * RANK)


def far_total(values):
    pair_total = lax.psum(values, "narrow")
    return pair_total + partner(pair_total, "wide", 0)


def body(
    moments,
    up_0,
    up_1,
    up_2,
    up_3,
    couple_0,
    couple_1,
    couple_2,
    couple_3,
    couple_4,
    sources_0,
    sources_1,
    sources_2,
    sources_3,
    sources_4,
    counts_0,
    counts_1,
    counts_2,
    counts_3,
    counts_4,
):
    transfers = [up_0, up_1, up_2, up_3]
    couplings = [couple_0, couple_1, couple_2, couple_3]
    source_lists = [sources_0, sources_1, sources_2, sources_3]
    count_lists = [counts_0, counts_1, counts_2, counts_3]
    position = lax.axis_index("wide") * lax.axis_size("narrow") + lax.axis_index("narrow")
    rounded = [moments.astype(jnp.bfloat16)]
    for level_index in range(3):
        terms = lift_terms(rounded[level_index], transfers[level_index])
        moment_next = terms.reshape(-1, 4, RHS * RANK).sum(axis=1)
        rounded.append(moment_next.astype(jnp.bfloat16))
    level_sizes = [rounded[level_index].shape[0] for level_index in range(4)]
    windows = []
    firsts = []
    for level_index in range(4):
        level_rows, level_first = window_rows(rounded[level_index], position)
        windows.append(level_rows)
        firsts.append(level_first)
    far_terms = [
        far_split(
            windows[level_index],
            firsts[level_index],
            level_sizes[level_index],
            couplings[level_index],
            source_lists[level_index],
            count_lists[level_index],
        )
        for level_index in range(4)
    ]
    child_term = lift_terms(rounded[3], up_3)
    slot_count = couple_4.shape[0]
    slot_global = position * slot_count + jnp.arange(slot_count, dtype=jnp.int32)
    target = slot_global // LIST
    all_terms = lax.all_gather(child_term, ("wide", "narrow"), axis=0, tiled=True)
    top_rounded = all_terms.reshape(-1, 4, RHS * RANK).sum(axis=1).astype(jnp.bfloat16)
    picked = jnp.take(top_rounded, sources_4, axis=0)
    valid = slot_global % LIST < jnp.take(counts_4, target)
    picked = jnp.where(valid[:, None], picked, jnp.zeros_like(picked))
    partial_value = jnp.einsum(
        "jrk,jkq->rq",
        picked.reshape(slot_count, RHS, RANK),
        couple_4.reshape(slot_count, RANK, RANK),
        preferred_element_type=jnp.float32,
    )
    partial_value = partial_value.reshape(1, RHS * RANK)
    parent_field = far_total(partial_value)
    field_rows = lower_terms(far_terms[3], parent_field, up_3)
    for level_index in (2, 1, 0):
        field_rows = lower_terms(far_terms[level_index], field_rows, transfers[level_index])
    return field_rows


def solution(mesh):
    placed = (
        P(("wide", "narrow"), None),
        P(("wide", "narrow"), None),
        P(("wide", "narrow"), None),
        P(("wide", "narrow"), None),
        P(("wide", "narrow"), None),
        P(("wide", "narrow"), None),
        P(("wide", "narrow"), None),
        P(("wide", "narrow"), None),
        P(("wide", "narrow"), None),
        P(("wide", "narrow"), None),
        P(("wide", "narrow")),
        P(("wide", "narrow")),
        P(("wide", "narrow")),
        P(("wide", "narrow")),
        P(("wide", "narrow")),
        P(("wide", "narrow")),
        P(("wide", "narrow")),
        P(("wide", "narrow")),
        P(("wide", "narrow")),
        P(),
    )
    return jax.shard_map(
        body, mesh=mesh, in_specs=placed, out_specs=P(("wide", "narrow"), None), check_vma=False
    )
```

profile of v0, /device:TPU:1, one launch (start us, length us, event | category | flops | bytes accessed | tf_op | source)
XLA Modules:
  0.0 577.8 jit_solution(14454545417403793646)
XLA Ops:
  12.6 3.3 collective-permute-start.29
  15.9 4.0 collective-permute-start.28
  19.9 3.3 collective-permute-start.27
  27.1 318.5 %all-gather = f32[128,1,1024]{2,1,0:T(1,128)S(1)} all-gather(f32[1,1,1024]{2,1,0:T(1,128)S(1)} %reshape.455), channel_id=1, replica_groups=mesh['wide'=64,'narrow'=2] {'wide','narrow'}, dimensions={0}, use_global_device_ids=true | all-gather | bytes 528384 | tf_op jit(solution)/shard_map/all_gather | solution.py:137
  353.0 5.3 psum.7
  361.0 2.9 reshape.392
  363.9 11.0 %reshape.390 = bf16[16,28,64,64]{3,2,1,0:T(8,128)(2,1)} reshape(bf16[448,4096]{1,0:T(8,128)(2,1)} %param.26) | data formatting | bytes 7340032 | tf_op jit(solution)/shard_map/reshape | solution.py:72
  375.0 40.3 %reshape.387 = bf16[64,28,64,64]{3,2,1,0:T(8,128)(2,1)} reshape(bf16[1792,4096]{1,0:T(8,128)(2,1)} %param.25) | data formatting | bytes 29360128 | tf_op jit(solution)/shard_map/reshape | solution.py:72
  417.9 6.2 %collective-permute-start.21 = (bf16[4,1024]{1,0:T(4,128)(2,1)S(1)}, bf16[4,1024]{1,0:T(4,128)(2,1)S(1)}, u32[]{:S(2)}, u32[]{:S(2)}) collective-permute-start(bf16[4,1024]{1,0:T(4,128)(2,1)S(1)} %reduce_sum.32), channel_id=1, source_target_pairs={{2,0},{3,1},{4,2},{5,3},{6,4},{7,5},{8,6},{9,7},{10,8},{11,9},{12,... | collective-permute-start | bytes 24584 | tf_op jit(solution)/shard_map/ppermute | solution.py:15
  428.3 5.4 collective-permute-start.19
  433.8 5.0 collective-permute-start.18
  438.9 6.4 %collective-permute-start.17 = (bf16[4,1024]{1,0:T(4,128)(2,1)S(1)}, bf16[4,1024]{1,0:T(4,128)(2,1)S(1)}, u32[]{:S(2)}, u32[]{:S(2)}) collective-permute-start(bf16[4,1024]{1,0:T(4,128)(2,1)S(1)} %reduce_sum.32), channel_id=1, source_target_pairs={{0,3},{1,4},{2,5},{3,6},{4,7},{5,8},{6,9},{7,10},{8,11},{9,12},{10... | collective-permute-start | bytes 24584 | tf_op jit(solution)/shard_map/ppermute | solution.py:15
  449.4 3.8 collective-permute-start.5
  453.2 6.6 %collective-permute-start.1 = (bf16[64,1024]{1,0:T(8,128)(2,1)}, bf16[64,1024]{1,0:T(8,128)(2,1)}, u32[]{:S(2)}, u32[]{:S(2)}) collective-permute-start(bf16[64,1024]{1,0:T(8,128)(2,1)} %convert_element_type.60), channel_id=1, source_target_pairs={{0,3},{1,4},{2,5},{3,6},{4,7},{5,8},{6,9},{7,10},{8,11},{9,12},{10... | collective-permute-start | bytes 393224 | tf_op jit(solution)/shard_map/ppermute | solution.py:15
  459.8 5.1 collective-permute-start.8
  469.2 2.4 collective-permute-start.9
  472.9 3.6 collective-permute-start.10
  477.8 4.8 collective-permute-start.11
  484.8 3.9 collective-permute-start.12
  493.1 4.8 collective-permute-done.13
  499.2 5.7 collective-permute-done.14
  506.2 6.0 %collective-permute-done.15 = bf16[16,1024]{1,0:T(8,128)(2,1)S(1)} collective-permute-done((bf16[16,1024]{1,0:T(8,128)(2,1)}, bf16[16,1024]{1,0:T(8,128)(2,1)S(1)}, u32[]{:S(2)}, u32[]{:S(2)}) %collective-permute-start.15) | collective-permute-done | bytes 32800 | tf_op jit(solution)/shard_map/ppermute | solution.py:15
  512.2 4.3 collective-permute-start
  518.6 2.1 gather.33
  520.7 5.0 fusion.24
  526.7 3.2 collective-permute-start.2
  529.9 3.1 collective-permute-start.3
  533.9 4.0 collective-permute-start.4
  538.0 4.4 collective-permute-done.4
  545.2 6.6 %gather_fusion = bf16[1792,1024]{1,0:T(8,128)(2,1)} fusion(bf16[576,1024]{1,0:T(8,128)(2,1)S(1)} %constant_dynamic-update-slice_fusion, s32[2048]{0:T(1024)S(1)} %pad_clamp_fusion), kind=kCustom, calls=%fused_computation | custom fusion | bytes 7347200 | tf_op jit(solution)/shard_map/jit(_take)/gather | solution.py:65
  551.8 10.4 %gather.31 = bf16[64,28,16,64]{3,2,1,0:T(8,128)(2,1)} reshape(bf16[1792,1024]{1,0:T(8,128)(2,1)} %gather_fusion) | data formatting | bytes 7340032 | tf_op jit(solution)/shard_map/jit(_take)/gather | solution.py:65
  562.2 14.7 %fusion.15 = f32[64,16,64]{2,1,0:T(8,128)S(1)} fusion(f32[64,16,64]{2,1,0:T(8,128)S(1)} %fusion.63, bf16[64,28,64,64]{3,2,1,0:T(8,128)(2,1)} %reshape.387, bf16[64,28,16,64]{3,2,1,0:T(8,128)(2,1)} %gather.31, pred[64,28]{1,0:T(8,128)(4,1)S(1)} %broadcast_in_dim.149, pred[64,28]{1,0:T(8,128)(4,1)S(1)} %copy-done.7), kind=kOutput, calls=%fused_computation.19 | convolution fusion | flops 238616576 | bytes 18877952 | tf_op jit(solution)/shard_map/tjrk,tjkq->trq/dot_general | solution.py:69
  (168 shorter events, 60.2 us)
Async XLA Ops:
  10.0 338.5 %collective-permute-start.31 = (bf16[1,1024]{1,0:T(2,128)(2,1)S(1)}, bf16[1,1024]{1,0:T(2,128)(2,1)S(1)}, u32[]{:S(2)}, u32[]{:S(2)}) collective-permute-start(bf16[1,1024]{1,0:T(2,128)(2,1)S(1)} %convert_element_type.66), channel_id=1, source_target_pairs={{4,0},{5,1},{6,2},{7,3},{8,4},{9,5},{10,6},{11,7},{12,8},{13,9},{1... | collective-permute-start | bytes 6152 | tf_op jit(solution)/shard_map/ppermute | solution.py:15
  11.3 339.1 %collective-permute-start.30 = (bf16[1,1024]{1,0:T(2,128)(2,1)S(1)}, bf16[1,1024]{1,0:T(2,128)(2,1)S(1)}, u32[]{:S(2)}, u32[]{:S(2)}) collective-permute-start(bf16[1,1024]{1,0:T(2,128)(2,1)S(1)} %convert_element_type.66), channel_id=1, source_target_pairs={{3,0},{4,1},{5,2},{6,3},{7,4},{8,5},{9,6},{10,7},{11,8},{12,9},{13... | collective-permute-start | bytes 6152 | tf_op jit(solution)/shard_map/ppermute | solution.py:15
  12.6 339.1 %collective-permute-start.29 = (bf16[1,1024]{1,0:T(2,128)(2,1)S(1)}, bf16[1,1024]{1,0:T(2,128)(2,1)S(1)}, u32[]{:S(2)}, u32[]{:S(2)}) collective-permute-start(bf16[1,1024]{1,0:T(2,128)(2,1)S(1)} %convert_element_type.66), channel_id=1, source_target_pairs={{2,0},{3,1},{4,2},{5,3},{6,4},{7,5},{8,6},{9,7},{10,8},{11,9},{12,... | collective-permute-start | bytes 6152 | tf_op jit(solution)/shard_map/ppermute | solution.py:15
  15.9 399.4 %collective-permute-start.28 = (bf16[1,1024]{1,0:T(2,128)(2,1)S(1)}, bf16[1,1024]{1,0:T(2,128)(2,1)S(1)}, u32[]{:S(2)}, u32[]{:S(2)}) collective-permute-start(bf16[1,1024]{1,0:T(2,128)(2,1)S(1)} %convert_element_type.66), channel_id=1, source_target_pairs={{1,0},{2,1},{3,2},{4,3},{5,4},{6,5},{7,6},{8,7},{9,8},{10,9},{11,1... | collective-permute-start | bytes 6152 | tf_op jit(solution)/shard_map/ppermute | solution.py:15
  19.9 396.7 %collective-permute-start.27 = (bf16[1,1024]{1,0:T(2,128)(2,1)S(1)}, bf16[1,1024]{1,0:T(2,128)(2,1)S(1)}, u32[]{:S(2)}, u32[]{:S(2)}) collective-permute-start(bf16[1,1024]{1,0:T(2,128)(2,1)S(1)} %convert_element_type.66), channel_id=1, source_target_pairs={{0,1},{1,2},{2,3},{3,4},{4,5},{5,6},{6,7},{7,8},{8,9},{9,10},{10,1... | collective-permute-start | bytes 6152 | tf_op jit(solution)/shard_map/ppermute | solution.py:15
  348.4 69.5 %collective-permute-start.26 = (bf16[1,1024]{1,0:T(2,128)(2,1)S(1)}, bf16[1,1024]{1,0:T(2,128)(2,1)S(1)}, u32[]{:S(2)}, u32[]{:S(2)}) collective-permute-start(bf16[1,1024]{1,0:T(2,128)(2,1)S(1)} %convert_element_type.66), channel_id=1, source_target_pairs={{0,2},{1,3},{2,4},{3,5},{4,6},{5,7},{6,8},{7,9},{8,10},{9,11},{10,... | collective-permute-start | bytes 6152 | tf_op jit(solution)/shard_map/ppermute | solution.py:15
  350.4 73.7 %collective-permute-start.25 = (bf16[1,1024]{1,0:T(2,128)(2,1)S(1)}, bf16[1,1024]{1,0:T(2,128)(2,1)S(1)}, u32[]{:S(2)}, u32[]{:S(2)}) collective-permute-start(bf16[1,1024]{1,0:T(2,128)(2,1)S(1)} %convert_element_type.66), channel_id=1, source_target_pairs={{0,3},{1,4},{2,5},{3,6},{4,7},{5,8},{6,9},{7,10},{8,11},{9,12},{10... | collective-permute-start | bytes 6152 | tf_op jit(solution)/shard_map/ppermute | solution.py:15
  351.7 74.4 %collective-permute-start.24 = (bf16[1,1024]{1,0:T(2,128)(2,1)S(1)}, bf16[1,1024]{1,0:T(2,128)(2,1)S(1)}, u32[]{:S(2)}, u32[]{:S(2)}) collective-permute-start(bf16[1,1024]{1,0:T(2,128)(2,1)S(1)} %convert_element_type.66), channel_id=1, source_target_pairs={{0,4},{1,5},{2,6},{3,7},{4,8},{5,9},{6,10},{7,11},{8,12},{9,13},{1... | collective-permute-start | bytes 6152 | tf_op jit(solution)/shard_map/ppermute | solution.py:15
  415.3 18.5 %collective-permute-start.23 = (bf16[4,1024]{1,0:T(4,128)(2,1)S(1)}, bf16[4,1024]{1,0:T(4,128)(2,1)S(1)}, u32[]{:S(2)}, u32[]{:S(2)}) collective-permute-start(bf16[4,1024]{1,0:T(4,128)(2,1)S(1)} %reduce_sum.32), channel_id=1, source_target_pairs={{4,0},{5,1},{6,2},{7,3},{8,4},{9,5},{10,6},{11,7},{12,8},{13,9},{1... | collective-permute-start | bytes 24584 | tf_op jit(solution)/shard_map/ppermute | solution.py:15
  416.6 22.3 %collective-permute-start.22 = (bf16[4,1024]{1,0:T(4,128)(2,1)S(1)}, bf16[4,1024]{1,0:T(4,128)(2,1)S(1)}, u32[]{:S(2)}, u32[]{:S(2)}) collective-permute-start(bf16[4,1024]{1,0:T(4,128)(2,1)S(1)} %reduce_sum.32), channel_id=1, source_target_pairs={{3,0},{4,1},{5,2},{6,3},{7,4},{8,5},{9,6},{10,7},{11,8},{12,9},{13... | collective-permute-start | bytes 24584 | tf_op jit(solution)/shard_map/ppermute | solution.py:15
  417.9 27.3 %collective-permute-start.21 = (bf16[4,1024]{1,0:T(4,128)(2,1)S(1)}, bf16[4,1024]{1,0:T(4,128)(2,1)S(1)}, u32[]{:S(2)}, u32[]{:S(2)}) collective-permute-start(bf16[4,1024]{1,0:T(4,128)(2,1)S(1)} %reduce_sum.32), channel_id=1, source_target_pairs={{2,0},{3,1},{4,2},{5,3},{6,4},{7,5},{8,6},{9,7},{10,8},{11,9},{12,... | collective-permute-start | bytes 24584 | tf_op jit(solution)/shard_map/ppermute | solution.py:15
  424.1 22.7 %collective-permute-start.20 = (bf16[4,1024]{1,0:T(4,128)(2,1)S(1)}, bf16[4,1024]{1,0:T(4,128)(2,1)S(1)}, u32[]{:S(2)}, u32[]{:S(2)}) collective-permute-start(bf16[4,1024]{1,0:T(4,128)(2,1)S(1)} %reduce_sum.32), channel_id=1, source_target_pairs={{1,0},{2,1},{3,2},{4,3},{5,4},{6,5},{7,6},{8,7},{9,8},{10,9},{11,1... | collective-permute-start | bytes 24584 | tf_op jit(solution)/shard_map/ppermute | solution.py:15
  428.3 19.8 %collective-permute-start.19 = (bf16[4,1024]{1,0:T(4,128)(2,1)S(1)}, bf16[4,1024]{1,0:T(4,128)(2,1)S(1)}, u32[]{:S(2)}, u32[]{:S(2)}) collective-permute-start(bf16[4,1024]{1,0:T(4,128)(2,1)S(1)} %reduce_sum.32), channel_id=1, source_target_pairs={{0,1},{1,2},{2,3},{3,4},{4,5},{5,6},{6,7},{7,8},{8,9},{9,10},{10,1... | collective-permute-start | bytes 24584 | tf_op jit(solution)/shard_map/ppermute | solution.py:15
  433.8 15.6 %collective-permute-start.18 = (bf16[4,1024]{1,0:T(4,128)(2,1)S(1)}, bf16[4,1024]{1,0:T(4,128)(2,1)S(1)}, u32[]{:S(2)}, u32[]{:S(2)}) collective-permute-start(bf16[4,1024]{1,0:T(4,128)(2,1)S(1)} %reduce_sum.32), channel_id=1, source_target_pairs={{0,2},{1,3},{2,4},{3,5},{4,6},{5,7},{6,8},{7,9},{8,10},{9,11},{10,... | collective-permute-start | bytes 24584 | tf_op jit(solution)/shard_map/ppermute | solution.py:15
  438.9 14.3 %collective-permute-start.17 = (bf16[4,1024]{1,0:T(4,128)(2,1)S(1)}, bf16[4,1024]{1,0:T(4,128)(2,1)S(1)}, u32[]{:S(2)}, u32[]{:S(2)}) collective-permute-start(bf16[4,1024]{1,0:T(4,128)(2,1)S(1)} %reduce_sum.32), channel_id=1, source_target_pairs={{0,3},{1,4},{2,5},{3,6},{4,7},{5,8},{6,9},{7,10},{8,11},{9,12},{10... | collective-permute-start | bytes 24584 | tf_op jit(solution)/shard_map/ppermute | solution.py:15
  445.2 14.5 %collective-permute-start.16 = (bf16[4,1024]{1,0:T(4,128)(2,1)S(1)}, bf16[4,1024]{1,0:T(4,128)(2,1)S(1)}, u32[]{:S(2)}, u32[]{:S(2)}) collective-permute-start(bf16[4,1024]{1,0:T(4,128)(2,1)S(1)} %reduce_sum.32), channel_id=1, source_target_pairs={{0,4},{1,5},{2,6},{3,7},{4,8},{5,9},{6,10},{7,11},{8,12},{9,13},{1... | collective-permute-start | bytes 24584 | tf_op jit(solution)/shard_map/ppermute | solution.py:15
  446.8 97.5 %collective-permute-start.7 = (bf16[64,1024]{1,0:T(8,128)(2,1)}, bf16[64,1024]{1,0:T(8,128)(2,1)}, u32[]{:S(2)}, u32[]{:S(2)}) collective-permute-start(bf16[64,1024]{1,0:T(8,128)(2,1)} %convert_element_type.60), channel_id=1, source_target_pairs={{4,0},{5,1},{6,2},{7,3},{8,4},{9,5},{10,6},{11,7},{12,8},{13,9},{1... | collective-permute-start | bytes 393224 | tf_op jit(solution)/shard_map/ppermute | solution.py:15
  448.1 95.3 %collective-permute-start.6 = (bf16[64,1024]{1,0:T(8,128)(2,1)}, bf16[64,1024]{1,0:T(8,128)(2,1)}, u32[]{:S(2)}, u32[]{:S(2)}) collective-permute-start(bf16[64,1024]{1,0:T(8,128)(2,1)} %convert_element_type.60), channel_id=1, source_target_pairs={{3,0},{4,1},{5,2},{6,3},{7,4},{8,5},{9,6},{10,7},{11,8},{12,9},{13... | collective-permute-start | bytes 393224 | tf_op jit(solution)/shard_map/ppermute | solution.py:15
  449.4 93.0 %collective-permute-start.5 = (bf16[64,1024]{1,0:T(8,128)(2,1)}, bf16[64,1024]{1,0:T(8,128)(2,1)}, u32[]{:S(2)}, u32[]{:S(2)}) collective-permute-start(bf16[64,1024]{1,0:T(8,128)(2,1)} %convert_element_type.60), channel_id=1, source_target_pairs={{2,0},{3,1},{4,2},{5,3},{6,4},{7,5},{8,6},{9,7},{10,8},{11,9},{12,... | collective-permute-start | bytes 393224 | tf_op jit(solution)/shard_map/ppermute | solution.py:15
  453.2 76.7 %collective-permute-start.1 = (bf16[64,1024]{1,0:T(8,128)(2,1)}, bf16[64,1024]{1,0:T(8,128)(2,1)}, u32[]{:S(2)}, u32[]{:S(2)}) collective-permute-start(bf16[64,1024]{1,0:T(8,128)(2,1)} %convert_element_type.60), channel_id=1, source_target_pairs={{0,3},{1,4},{2,5},{3,6},{4,7},{5,8},{6,9},{7,10},{8,11},{9,12},{10... | collective-permute-start | bytes 393224 | tf_op jit(solution)/shard_map/ppermute | solution.py:15
  459.8 9.4 %collective-permute-start.8 = (bf16[16,1024]{1,0:T(8,128)(2,1)}, bf16[16,1024]{1,0:T(8,128)(2,1)}, u32[]{:S(2)}, u32[]{:S(2)}) collective-permute-start(bf16[16,1024]{1,0:T(8,128)(2,1)} %reduce_sum.27), channel_id=1, source_target_pairs={{0,4},{1,5},{2,6},{3,7},{4,8},{5,9},{6,10},{7,11},{8,12},{9,13},{1... | collective-permute-start | bytes 98312 | tf_op jit(solution)/shard_map/ppermute | solution.py:15
  469.2 3.7 collective-permute-start.9
  472.9 4.9 collective-permute-start.10
  477.8 6.9 %collective-permute-start.11 = (bf16[16,1024]{1,0:T(8,128)(2,1)}, bf16[16,1024]{1,0:T(8,128)(2,1)S(1)}, u32[]{:S(2)}, u32[]{:S(2)}) collective-permute-start(bf16[16,1024]{1,0:T(8,128)(2,1)} %reduce_sum.27), channel_id=1, source_target_pairs={{0,1},{1,2},{2,3},{3,4},{4,5},{5,6},{6,7},{7,8},{8,9},{9,10},{10,1... | collective-permute-start | bytes 98312 | tf_op jit(solution)/shard_map/ppermute | solution.py:15
  484.8 6.4 %collective-permute-start.12 = (bf16[16,1024]{1,0:T(8,128)(2,1)}, bf16[16,1024]{1,0:T(8,128)(2,1)S(1)}, u32[]{:S(2)}, u32[]{:S(2)}) collective-permute-start(bf16[16,1024]{1,0:T(8,128)(2,1)} %reduce_sum.27), channel_id=1, source_target_pairs={{1,0},{2,1},{3,2},{4,3},{5,4},{6,5},{7,6},{8,7},{9,8},{10,9},{11,1... | collective-permute-start | bytes 98312 | tf_op jit(solution)/shard_map/ppermute | solution.py:15
  491.1 6.8 %collective-permute-start.13 = (bf16[16,1024]{1,0:T(8,128)(2,1)}, bf16[16,1024]{1,0:T(8,128)(2,1)S(1)}, u32[]{:S(2)}, u32[]{:S(2)}) collective-permute-start(bf16[16,1024]{1,0:T(8,128)(2,1)} %reduce_sum.27), channel_id=1, source_target_pairs={{2,0},{3,1},{4,2},{5,3},{6,4},{7,5},{8,6},{9,7},{10,8},{11,9},{12,... | collective-permute-start | bytes 98312 | tf_op jit(solution)/shard_map/ppermute | solution.py:15
  497.9 7.0 %collective-permute-start.14 = (bf16[16,1024]{1,0:T(8,128)(2,1)}, bf16[16,1024]{1,0:T(8,128)(2,1)S(1)}, u32[]{:S(2)}, u32[]{:S(2)}) collective-permute-start(bf16[16,1024]{1,0:T(8,128)(2,1)} %reduce_sum.27), channel_id=1, source_target_pairs={{3,0},{4,1},{5,2},{6,3},{7,4},{8,5},{9,6},{10,7},{11,8},{12,9},{13... | collective-permute-start | bytes 98312 | tf_op jit(solution)/shard_map/ppermute | solution.py:15
  504.9 7.3 %collective-permute-start.15 = (bf16[16,1024]{1,0:T(8,128)(2,1)}, bf16[16,1024]{1,0:T(8,128)(2,1)S(1)}, u32[]{:S(2)}, u32[]{:S(2)}) collective-permute-start(bf16[16,1024]{1,0:T(8,128)(2,1)} %reduce_sum.27), channel_id=1, source_target_pairs={{4,0},{5,1},{6,2},{7,3},{8,4},{9,5},{10,6},{11,7},{12,8},{13,9},{1... | collective-permute-start | bytes 98312 | tf_op jit(solution)/shard_map/ppermute | solution.py:15
  512.2 14.5 %collective-permute-start = (bf16[64,1024]{1,0:T(8,128)(2,1)}, bf16[64,1024]{1,0:T(8,128)(2,1)S(1)}, u32[]{:S(2)}, u32[]{:S(2)}) collective-permute-start(bf16[64,1024]{1,0:T(8,128)(2,1)} %convert_element_type.60), channel_id=1, source_target_pairs={{0,4},{1,5},{2,6},{3,7},{4,8},{5,9},{6,10},{7,11},{8,12},{9,13},{1... | collective-permute-start | bytes 393224 | tf_op jit(solution)/shard_map/ppermute | solution.py:15
  526.7 7.2 %collective-permute-start.2 = (bf16[64,1024]{1,0:T(8,128)(2,1)}, bf16[64,1024]{1,0:T(8,128)(2,1)S(1)}, u32[]{:S(2)}, u32[]{:S(2)}) collective-permute-start(bf16[64,1024]{1,0:T(8,128)(2,1)} %convert_element_type.60), channel_id=1, source_target_pairs={{0,2},{1,3},{2,4},{3,5},{4,6},{5,7},{6,8},{7,9},{8,10},{9,11},{10,... | collective-permute-start | bytes 393224 | tf_op jit(solution)/shard_map/ppermute | solution.py:15
  529.9 8.0 %collective-permute-start.3 = (bf16[64,1024]{1,0:T(8,128)(2,1)}, bf16[64,1024]{1,0:T(8,128)(2,1)S(1)}, u32[]{:S(2)}, u32[]{:S(2)}) collective-permute-start(bf16[64,1024]{1,0:T(8,128)(2,1)} %convert_element_type.60), channel_id=1, source_target_pairs={{0,1},{1,2},{2,3},{3,4},{4,5},{5,6},{6,7},{7,8},{8,9},{9,10},{10,1... | collective-permute-start | bytes 393224 | tf_op jit(solution)/shard_map/ppermute | solution.py:15
  533.9 8.5 %collective-permute-start.4 = (bf16[64,1024]{1,0:T(8,128)(2,1)}, bf16[64,1024]{1,0:T(8,128)(2,1)S(1)}, u32[]{:S(2)}, u32[]{:S(2)}) collective-permute-start(bf16[64,1024]{1,0:T(8,128)(2,1)} %convert_element_type.60), channel_id=1, source_target_pairs={{1,0},{2,1},{3,2},{4,3},{5,4},{6,5},{7,6},{8,7},{9,8},{10,9},{11,1... | collective-permute-start | bytes 393224 | tf_op jit(solution)/shard_map/ppermute | solution.py:15
  (18 other events, 889.3 us)
where the time goes:
time: 581 us; the launch traced here: 578 us
  blocking collectives  324 us (56%)
  starting transfers between devices  98.5 us (17%)
  local copies, waits for them, and re-layouts  96.5 us (17%)
  waiting for transfers between devices  26.5 us (5%)
  matrix products  24.7 us (4%)
  other arithmetic  6.25 us (1%)
    all_gather x1, blocking collectives, body(): lax.all_gather(child_term, ('wide', 'narrow'), axis=0, tiled=True)  319 us
    ppermute x32, starting transfers between devices, passed_along(): return lax.ppermute(array, axis, pairs)  98.4 us
    reshape x3, local copies, waits for them, and re-layouts, far_split(): couple.reshape(per_device, LIST, RANK, RANK)  54.3 us
    ppermute x32, waiting for transfers between devices, passed_along(): return lax.ppermute(array, axis, pairs)  26.5 us
    gather x7, local copies, waits for them, and re-layouts, far_split(): picked = jnp.take(gathered, local_index, axis=0)  23.8 us
    dot_general x4, matrix products, far_split(): jnp.einsum('tjrk,tjkq->trq', picked.reshape(per_device, LIST, RHS, RANK),...  22.5 us
  transfers between devices with their start and end apart: 33, of which 8 were waited for; matrix products, arithmetic and copies ran while one was open for 15% of the time, Pallas kernels for 0%

commit v1 on v0

v1 whole, which is shorter than its diff:
```python
import functools

import jax
import jax.numpy as jnp
from jax import lax
from jax.experimental import pallas as pl
from jax.experimental.pallas import tpu as pltpu
from jax.sharding import PartitionSpec as P

RANK = 64
RHS = 16
LIST = 28
REACH = 4
WIDTH = RHS * RANK
BLOCK = RANK * RANK
LANES = 128
SUPER = 4 * LIST
GROUPS = SUPER // 16
WINDOW = 2 * REACH + 1
MESH = pl.DeviceIdType.MESH
BF16 = jnp.bfloat16
F32 = jnp.float32

TOUCH = [
    [b for b in range(4) if b * LIST < 16 * g + 16 and (b + 1) * LIST > 16 * g]
    for g in range(GROUPS)
]


def low_lanes(shape):
    return lax.broadcasted_iota(jnp.int32, shape, 1) < RANK


def swap_halves(value):
    return pltpu.roll(value, RANK, 1)


def kernel(
    devices,
    moments,
    up_0,
    up_1,
    up_2,
    up_3,
    couple_0,
    couple_1,
    couple_2,
    couple_3,
    couple_4,
    sources_0,
    sources_1,
    sources_2,
    sources_3,
    sources_4,
    counts_0,
    counts_1,
    counts_2,
    counts_3,
    counts_4,
    out,
    mom,
    u0,
    u1,
    u2,
    u3,
    c0,
    c1,
    c2,
    c3,
    c4,
    s0,
    pad3,
    pad4,
    tiles,
    rows_b,
    perm,
    win_a,
    win_b,
    up_f,
    up_b,
    lines,
    index,
    gathered,
    far,
    terms,
    top,
    parts,
    load_sem,
    send_a,
    recv_a,
    send_b,
    recv_b,
    send_t,
    recv_t,
    send_m,
    recv_m,
    send_f,
    recv_f,
):
    tops = devices // 4
    me = lax.axis_index("wide") * 2 + lax.axis_index("narrow")
    member = lax.rem(me, 4)
    group = lax.div(me, 4)

    def place(position):
        return (lax.div(position, 2), lax.rem(position, 2))

    def shifted(by):
        return lax.rem(me + by + devices, devices)

    def mate(v):
        return group * 4 + lax.rem(member + v, 4)

    offsets = [o for o in range(-REACH, REACH + 1) if o != 0]

    barrier = pltpu.get_barrier_semaphore()
    for o in offsets:
        pl.semaphore_signal(barrier, inc=1, device_id=place(shifted(o)), device_id_type=MESH)

    def greet(u, carry):
        pl.semaphore_signal(
            barrier, inc=1, device_id=place(shifted(4 * u)), device_id_type=MESH
        )
        return carry

    lax.fori_loop(2, tops - 1, greet, 0)

    loads = [
        (moments, mom),
        (up_0, u0),
        (up_1, u1),
        (up_2, u2),
        (up_3, u3),
        (sources_0, s0),
        (couple_3, c3),
        (couple_4, c4),
        (couple_0, c0),
        (couple_1, c1),
        (couple_2, c2),
    ]
    copies = [
        pltpu.make_async_copy(src, dst, load_sem.at[n]) for n, (src, dst) in enumerate(loads)
    ]
    for copy in copies:
        copy.start()

    def build_perm(j, carry):
        a = lax.broadcasted_iota(jnp.int32, (LANES, WIDTH), 0)
        b = lax.broadcasted_iota(jnp.int32, (LANES, WIDTH), 1)
        wanted = (a % RANK) * RHS + (a // RANK) * 8 + j
        start = pl.multiple_of(j * LANES, LANES)
        perm[pl.ds(start, LANES), :] = jnp.where(wanted == b, 1.0, 0.0).astype(BF16)
        return carry

    lax.fori_loop(0, 8, build_perm, 0)

    copies[0].wait()
    win_a[REACH] = jnp.dot(
        mom[...].astype(BF16), perm[...], preferred_element_type=F32
    ).astype(BF16)

    pl.semaphore_wait(barrier, len(offsets) + tops - 3)

    def exchange(window, send, recv):
        return [
            pltpu.make_async_remote_copy(
                src_ref=window.at[REACH],
                dst_ref=window.at[REACH - o],
                send_sem=send.at[n],
                recv_sem=recv.at[REACH - o],
                device_id=place(shifted(o)),
                device_id_type=MESH,
            )
            for n, o in enumerate(offsets)
        ]

    sends_a = exchange(win_a, send_a, recv_a)
    for copy in sends_a:
        copy.start()

    for n in range(1, 5):
        copies[n].wait()
    bases = [0, 64, 80, 84]

    def spread(m, carry):
        lane = pl.ds(pl.multiple_of(m * LANES, LANES), LANES)
        for source, base, boxes in ((u0, 0, 64), (u1, 64, 16), (u2, 80, 4), (u3, 84, 1)):
            block = source[:, lane].astype(F32)
            other = swap_halves(block)
            step = min(boxes, 8)
            for first in range(0, boxes, step):
                for kp, value in ((0, block), (1, other)):
                    start = (base + first) * RANK + 2 * m + kp
                    piece = value[first : first + step]
                    if step > 1:
                        up_f[pl.ds(start, step, stride=RANK), :] = piece
                    else:
                        up_f[pl.ds(start, 1), :] = piece
        return carry

    lax.fori_loop(0, 32, spread, 0)

    def narrowed(n, carry):
        rows = pl.ds(pl.multiple_of(n * 320, 320), 320)
        up_b[rows, :] = up_f[rows, :].astype(BF16)
        return carry

    lax.fori_loop(0, 17, narrowed, 0)

    for big in range(8):
        for j in range(8):
            tiles[pl.ds((big * 8 + j) * 8, 8), :] = mom[
                big * 8 : big * 8 + 8, j * LANES : (j + 1) * LANES
            ]

    low = low_lanes((8, LANES))

    def beside(first, second):
        even = jnp.where(low, first, swap_halves(second))
        odd = jnp.where(low, swap_halves(first), second)
        return jnp.concatenate([even, odd], axis=0)

    def lifted(children, base):
        left = beside(children[0], children[1])
        right = beside(children[2], children[3])
        rows = jnp.concatenate([left, right], axis=1).astype(BF16)
        product = jnp.dot(
            rows, up_b[base * RANK : (base + 4) * RANK, :], preferred_element_type=F32
        )
        return jnp.where(low, product[:8], swap_halves(product[8:]))

    def tile_of(box):
        return tiles[pl.ds((box // 8) * 64 + box % 8, 8, stride=8), :]

    level_1 = [lifted([tile_of(4 * p + c) for c in range(4)], 4 * p) for p in range(16)]
    level_2 = [lifted(level_1[4 * p : 4 * p + 4], 64 + 4 * p) for p in range(4)]
    level_3 = lifted(level_2, 80)
    alone = jnp.concatenate([level_3, swap_halves(level_3)], axis=0)[:, :RANK].astype(BF16)
    product = jnp.dot(alone, up_b[84 * RANK : 85 * RANK, :], preferred_element_type=F32)
    terms[0] = jnp.where(low, product[:8], swap_halves(product[8:]))

    def to_mates(buffer, send, recv):
        return [
            pltpu.make_async_remote_copy(
                src_ref=buffer.at[0],
                dst_ref=buffer.at[4 - v],
                send_sem=send.at[v],
                recv_sem=recv.at[4 - v],
                device_id=place(mate(v)),
                device_id_type=MESH,
            )
            for v in (1, 2, 3)
        ]

    sends_t = to_mates(terms, send_t, recv_t)
    for copy in sends_t:
        copy.start()

    rows_b[...] = jnp.zeros_like(rows_b)
    for row, value in enumerate(level_1 + level_2 + [level_3]):
        rows_b[pl.ds((row // 8) * 64 + row % 8, 8, stride=8), :] = value
    natural = jnp.concatenate(
        [
            jnp.concatenate(
                [rows_b[(big * 8 + j) * 8 : (big * 8 + j) * 8 + 8, :] for j in range(8)], axis=1
            )
            for big in range(4)
        ],
        axis=0,
    ).astype(BF16)
    win_b[REACH] = jnp.dot(natural, perm[...], preferred_element_type=F32).astype(BF16)
    sends_b = exchange(win_b, send_b, recv_b)
    for copy in sends_b:
        copy.start()

    copies[5].wait()
    first = me - REACH
    for j in range(14):
        lines[j : j + 1, :] = s0[pl.ds(j * LANES, LANES)].reshape(1, LANES) - first * 64
    lines[14:32, :] = jnp.zeros((18, LANES), jnp.int32)
    for j in range(4):
        length = min(LANES, 448 - j * LANES)
        local = sources_1[pl.ds(j * LANES, length)].reshape(1, length) - first * 16
        lines[14 + j : 15 + j, :length] = (local >> 4) * 32 + (local & 15)
    local = sources_2[...].reshape(1, 112) - first * 4
    lines[18:19, :112] = (local >> 2) * 32 + 16 + (local & 3)
    lines[19:20, :28] = (sources_3[...].reshape(1, 28) - first) * 32 + 20
    lines[20:21, :7] = (sources_4[...].reshape(1, 7) - group) & (tops - 1)
    columns = lines[...].T
    for j in range(21):
        index[j * LANES : (j + 1) * LANES, :] = jnp.broadcast_to(
            columns[:, j : j + 1], (LANES, LANES)
        )

    slot = lax.broadcasted_iota(jnp.int32, (SUPER, LANES), 0)

    def drop_invalid(base, counts):
        limit = counts[3] + 3 * LIST
        for b in (2, 1, 0):
            limit = jnp.where(slot < (b + 1) * LIST, counts[b] + b * LIST, limit)
        rows = pl.ds(base, SUPER)
        index[rows, :] = jnp.where(slot < limit, index[rows, :], -1)

    def drop_level(first_row, counts_ref, n):
        def step(n, carry):
            base = pl.multiple_of(first_row + n * SUPER, 16)
            drop_invalid(base, [counts_ref[4 * n + b] for b in range(4)])
            return carry

        lax.fori_loop(0, n, step, 0)

    drop_level(0, counts_0, 16)
    drop_level(1792, counts_1, 4)
    drop_level(2304, counts_2, 1)
    few = lax.broadcasted_iota(jnp.int32, (32, LANES), 0)
    index[2432:2464, :] = jnp.where(few < counts_3[0], index[2432:2464, :], -1)
    left = jnp.minimum(counts_4[group] - member * 7, 7)
    index[2560:2592, :] = jnp.where(few < left, index[2560:2592, :], -1)

    for copy in sends_t:
        copy.wait_recv()
    top[0] = (terms[0] + terms[1]) + (terms[2] + terms[3])

    def to_top(u):
        return pltpu.make_async_remote_copy(
            src_ref=top.at[0],
            dst_ref=top.at[tops - u],
            send_sem=send_m,
            recv_sem=recv_m,
            device_id=place(shifted(4 * u)),
            device_id_type=MESH,
        )

    def send_top(u, carry):
        to_top(u).start()
        return carry

    lax.fori_loop(1, tops, send_top, 0)

    def picked(start, count, sources, width):
        place_of = index[pl.ds(start, count), :]
        lane = lax.broadcasted_iota(jnp.int32, (count, LANES), 1)
        hot = [
            jnp.where(place_of == lane + first_lane, 1.0, 0.0).astype(BF16)[
                :, : min(LANES, width - first_lane)
            ]
            for first_lane in range(0, width, LANES)
        ]
        hot = jnp.concatenate(hot, axis=1) if len(hot) > 1 else hot[0]
        return jnp.dot(hot, sources, preferred_element_type=F32).astype(BF16)

    def gather(start, to, count, window, width):
        for piece in range(0, WIDTH, 256):
            sources = window[:, :, piece : piece + 256].reshape(width, 256)
            gathered[pl.ds(to, count), piece : piece + 256] = picked(
                start, count, sources, width
            )

    def turned(rows):
        stack = jnp.concatenate(
            [rows[:, i * LANES : (i + 1) * LANES] for i in range(8)], axis=0
        )
        across = stack.T
        return jnp.concatenate([across[32 * m : 32 * m + 32] for m in range(4)], axis=1)

    def stacked(rows):
        return jnp.concatenate(
            [
                rows[:, (4 * i + m) * LANES : (4 * i + m + 1) * LANES]
                for m in range(4)
                for i in range(8)
            ],
            axis=0,
        )

    def box_tile(value):
        a, b, c, d = (value[8 * n : 8 * n + 8] for n in range(4))
        return jnp.where(low, a, d) + swap_halves(jnp.where(low, b, c))

    def far_super(rows_from, couple, couple_from, far_from):
        totals = [None] * 4
        lane_slot = lax.broadcasted_iota(jnp.int32, (32, 512), 1) % 16
        for g in range(GROUPS):
            left = turned(gathered[pl.ds(rows_from + 16 * g, 16), :])
            right = stacked(couple[pl.ds(couple_from + 16 * g, 16), :])
            boxes = TOUCH[g]
            if len(boxes) == 2:
                border = boxes[1] * LIST - 16 * g
                zero = jnp.zeros_like(left)
                left = jnp.concatenate(
                    [
                        jnp.where(lane_slot < border, left, zero),
                        jnp.where(lane_slot < border, zero, left),
                    ],
                    axis=0,
                )
            value = jnp.dot(left, right, preferred_element_type=F32)
            for n, b in enumerate(boxes):
                part = value[32 * n : 32 * n + 32]
                totals[b] = part if totals[b] is None else totals[b] + part
        for b in range(4):
            far[pl.ds(far_from + 8 * b, 8), :] = box_tile(totals[b])

    for copy in sends_a:
        copy.wait_recv()

    def gather_0(n, carry):
        start = pl.multiple_of(n * 448, 448)
        gather(start, start, 448, win_a, WINDOW * 64)
        return carry

    lax.fori_loop(0, 4, gather_0, 0)
    copies[8].wait()

    def far_0(n, carry):
        start = pl.multiple_of(n * SUPER, SUPER)
        far_super(start, c0, start, pl.multiple_of(n * 32, 32))
        return carry

    lax.fori_loop(0, 16, far_0, 0)

    copies[6].wait()
    copies[7].wait()
    pad4[...] = jnp.zeros_like(pad4)
    pad4[0:7, :] = c4[...].astype(F32)
    pad3[...] = jnp.zeros_like(pad3)
    pad3[0:28, :] = c3[...].astype(F32)

    def all_top(n):
        return pltpu.make_async_copy(
            top.at[pl.ds(1, tops - 1)], top.at[pl.ds(1, tops - 1)], n
        )

    all_top(recv_m).wait()
    count = max(tops, 8)
    if tops < 8:
        tiles[0:512, :] = jnp.zeros((512, LANES), F32)
    for row in range(tops):
        tiles[pl.ds((row // 8) * 64 + row % 8, 8, stride=8), :] = top[row]
    natural = jnp.concatenate(
        [
            jnp.concatenate(
                [tiles[(big * 8 + j) * 8 : (big * 8 + j) * 8 + 8, :] for j in range(8)], axis=1
            )
            for big in range(count // 8)
        ],
        axis=0,
    ).astype(BF16)
    top_rows = jnp.dot(natural, perm[...], preferred_element_type=F32).astype(BF16)
    left = turned(picked(2560, 16, top_rows, count))
    right = stacked(pad4[...].astype(BF16))
    parts[0] = box_tile(jnp.dot(left, right, preferred_element_type=F32))
    sends_f = to_mates(parts, send_f, recv_f)
    for copy in sends_f:
        copy.start()

    for copy in sends_b:
        copy.wait_recv()
    copies[9].wait()
    copies[10].wait()
    gather(1792, 0, 448, win_b, WINDOW * 32)
    gather(2304, 448, SUPER, win_b, WINDOW * 32)
    gather(2432, 560, 32, win_b, WINDOW * 32)

    def far_1(n, carry):
        start = pl.multiple_of(n * SUPER, SUPER)
        far_super(start, c1, start, pl.multiple_of(512 + n * 32, 32))
        return carry

    lax.fori_loop(0, 4, far_1, 0)
    far_super(448, c2, 0, 640)
    total = None
    for g in range(2):
        left = turned(gathered[560 + 16 * g : 576 + 16 * g, :])
        right = stacked(pad3[16 * g : 16 * g + 16, :].astype(BF16))
        value = jnp.dot(left, right, preferred_element_type=F32)
        total = value if total is None else total + value
    far_3 = box_tile(total)

    def lowered(parent, base, boxes):
        rows = jnp.concatenate(
            [jnp.where(low, parent, 0.0), jnp.where(low, swap_halves(parent), 0.0)], axis=0
        ).astype(BF16)
        product = lax.dot_general(
            rows,
            up_b[base * RANK : (base + boxes) * RANK, :],
            (((1,), (1,)), ((), ())),
            preferred_element_type=F32,
        )
        result = []
        for pair in range(0, boxes, 2):
            even = product[:8, pair * RANK : pair * RANK + LANES]
            odd = product[8:, pair * RANK : pair * RANK + LANES]
            result.append(jnp.where(low, even, swap_halves(odd)))
            result.append(jnp.where(low, swap_halves(even), odd))
        return result

    for copy in sends_f:
        copy.wait_recv()
    field_4 = (parts[0] + parts[1]) + (parts[2] + parts[3])
    rows = jnp.concatenate(
        [jnp.where(low, field_4, 0.0), jnp.where(low, swap_halves(field_4), 0.0)], axis=0
    ).astype(BF16)
    product = lax.dot_general(
        rows,
        up_b[84 * RANK : 85 * RANK, :],
        (((1,), (1,)), ((), ())),
        preferred_element_type=F32,
    )
    product = jnp.concatenate([product, jnp.zeros_like(product)], axis=1)
    field_3 = far_3 + jnp.where(low, product[:8], swap_halves(product[8:]))
    down = lowered(field_3, 80, 4)
    field_2 = [far[640 + 8 * c : 648 + 8 * c, :] + down[c] for c in range(4)]
    field_1 = []
    for p in range(4):
        down = lowered(field_2[p], 64 + 4 * p, 4)
        for c in range(4):
            row = 512 + 8 * (4 * p + c)
            field_1.append(far[row : row + 8, :] + down[c])
    for p in range(16):
        down = lowered(field_1[p], 4 * p, 4)
        for c in range(4):
            box = 4 * p + c
            tiles[pl.ds((box // 8) * 64 + box % 8, 8, stride=8), :] = (
                far[8 * box : 8 * box + 8, :] + down[c]
            )
    for big in range(8):
        for j in range(8):
            row = (big * 8 + j) * 8
            out[big * 8 : big * 8 + 8, j * LANES : (j + 1) * LANES] = tiles[row : row + 8, :]

    for copy in sends_a + sends_b + sends_t + sends_f:
        copy.wait_send()
    all_top(send_m).wait()


def solution(mesh):
    devices = mesh.shape["wide"] * mesh.shape["narrow"]
    tops = devices // 4
    split = P(("wide", "narrow"), None)
    line = P(("wide", "narrow"))
    anywhere = pl.BlockSpec(memory_space=pl.ANY)
    scalars = pl.BlockSpec(memory_space=pltpu.SMEM)
    inside = pl.BlockSpec(memory_space=pltpu.VMEM)
    vmem = pltpu.VMEM
    dma = pltpu.SemaphoreType.DMA

    def body(*arrays):
        return pl.pallas_call(
            functools.partial(kernel, devices),
            out_shape=jax.ShapeDtypeStruct((64, WIDTH), F32),
            in_specs=[anywhere] * 11 + [inside] * 4 + [scalars] * 5,
            out_specs=pl.BlockSpec(memory_space=pltpu.VMEM),
            scratch_shapes=[
                vmem((64, WIDTH), F32),
                vmem((64, BLOCK), BF16),
                vmem((16, BLOCK), BF16),
                vmem((4, BLOCK), BF16),
                vmem((1, BLOCK), BF16),
                vmem((1792, BLOCK), BF16),
                vmem((448, BLOCK), BF16),
                vmem((112, BLOCK), BF16),
                vmem((28, BLOCK), BF16),
                vmem((7, BLOCK), BF16),
                vmem((1792,), jnp.int32),
                vmem((32, BLOCK), F32),
                vmem((16, BLOCK), F32),
                vmem((512, LANES), F32),
                vmem((256, LANES), F32),
                vmem((WIDTH, WIDTH), BF16),
                vmem((WINDOW, 64, WIDTH), BF16),
                vmem((WINDOW, 32, WIDTH), BF16),
                vmem((85 * RANK, LANES), F32),
                vmem((85 * RANK, LANES), BF16),
                vmem((32, LANES), jnp.int32),
                vmem((21 * LANES, LANES), jnp.int32),
                vmem((1792, WIDTH), BF16),
                vmem((84 * 8, LANES), F32),
                vmem((4, 8, LANES), F32),
                vmem((tops, 8, LANES), F32),
                vmem((4, 8, LANES), F32),
                dma((11,)),
                dma((2 * REACH,)),
                dma((WINDOW,)),
                dma((2 * REACH,)),
                dma((WINDOW,)),
                dma((4,)),
                dma((4,)),
                dma,
                dma,
                dma((4,)),
                dma((4,)),
            ],
            compiler_params=pltpu.CompilerParams(
                collective_id=0, has_side_effects=True, vmem_limit_bytes=56 * 1024 * 1024
            ),
        )(*arrays)

    return jax.shard_map(
        body,
        mesh=mesh,
        in_specs=(split,) * 10 + (line,) * 9 + (P(),),
        out_specs=split,
        check_vma=False,
    )
```

time: 581 us -> 47.4 us (0.08)
  blocking collectives: 324 us -> 0 us
  starting transfers between devices: 98.5 us -> 0 us
  local copies, waits for them, and re-layouts: 96.5 us -> 1.67 us
  Pallas kernels: 0 us -> 44.9 us
  waiting for transfers between devices: 26.5 us -> 0 us
  matrix products: 24.7 us -> 0 us
  other arithmetic: 6.25 us -> 0 us
    all_gather x1 -> x0, blocking collectives: 319 us -> none  [body(): lax.all_gather(child_term, ('wide', 'narrow'), axis=0, tiled=True)]
    ppermute x33 -> x0, starting transfers between devices: 98.5 us -> none  [the longest x32 98.4 us: passed_along(): return lax.ppermute(array, axis, pairs)]
    reshape x10 -> x0, local copies, waits for them, and re-layouts: 59.9 us -> none  [the longest x3 54.3 us: far_split(): couple.reshape(per_device, LIST, RANK, RANK)]
    pallas_call x0 -> x1, Pallas kernels: none -> 44.9 us  [body(): pl.pallas_call(functools.partial(kernel, devices), out_shape=jax.ShapeDty...]
    ppermute x33 -> x0, waiting for transfers between devices: 26.5 us -> none  [the longest x32 26.5 us: passed_along(): return lax.ppermute(array, axis, pairs)]
    gather x9 -> x0, local copies, waits for them, and re-layouts: 25 us -> none  [the longest x7 23.8 us: far_split(): picked = jnp.take(gathered, local_index, axis=0)]
    dot_general x13 -> x0, matrix products: 24.7 us -> none  [the longest x4 22.5 us: far_split(): jnp.einsum('tjrk,tjkq->trq', picked.reshape(per_device, LIST, RHS, RANK),...]
  transfers between devices with their start and end apart: 33 -> 0, of which waited for: 8 -> 0; matrix products, arithmetic and copies ran while one was open for 15% -> 0% of each run, Pallas kernels for 0% -> 0%
where the time goes in v1:
time: 47.4 us; the launch traced here: 47.2 us
  Pallas kernels  44.9 us (95%)
  local copies, waits for them, and re-layouts  1.67 us (4%)
  between operations  0.66 us (1%)
    pallas_call x1, Pallas kernels, body(): pl.pallas_call(functools.partial(kernel, devices), out_shape=jax.ShapeDty...  44.9 us
    unnamed x1, local copies, waits for them, and re-layouts  1.67 us

profile of v1, /device:TPU:1, one launch (start us, length us, event | category | flops | bytes accessed | tf_op | source)
XLA Modules:
  0.0 47.2 jit_solution(17360943396128564860)
XLA Ops:
  0.7 44.9 %shard_map.190 = f32[64,1024]{1,0:T(8,128)} custom-call(f32[64,1024]{1,0:T(8,128)} %moments.1, bf16[64,4096]{1,0:T(8,128)(2,1)} %up_0.1, bf16[16,4096]{1,0:T(8,128)(2,1)} %up_1.1, bf16[4,4096]{1,0:T(4,128)(2,1)} %up_2.1, bf16[1,4096]{1,0:T(2,128)(2,1)} %up_3.1, bf16[1792,4096]{1,0:T(8,128)(2,1)} %couple_0.1, bf16[448,4096]{1,0:T(8,128)(2,1)} %couple_1.1, ...), custom_call_target="tpu_custom_call" | custom-call | tf_op jit(solution)/shard_map/pallas_call | solution.py:549
  45.5 1.7 %copy.23 = f32[64,1024]{1,0:T(8,128)} copy(f32[64,1024]{1,0:T(8,128)} %shard_map.190) | data formatting | bytes 524288

commit v2 on v1

--- a/solution.py
+++ b/solution.py
@@ -15,16 +15,14 @@
 BLOCK = RANK * RANK
 LANES = 128
 SUPER = 4 * LIST
-GROUPS = SUPER // 16
+GROUP = 32
+WIDE = 2 * SUPER
+PIECES = 2
+PART = WIDTH // PIECES
 WINDOW = 2 * REACH + 1
 MESH = pl.DeviceIdType.MESH
 BF16 = jnp.bfloat16
 F32 = jnp.float32
-
-TOUCH = [
-    [b for b in range(4) if b * LIST < 16 * g + 16 and (b + 1) * LIST > 16 * g]
-    for g in range(GROUPS)
-]
 
 
 def low_lanes(shape):
@@ -63,9 +61,7 @@
     u1,
     u2,
     u3,
-    c0,
-    c1,
-    c2,
+    couples,
     c3,
     c4,
     s0,
@@ -80,6 +76,8 @@
     up_b,
     lines,
     index,
+    hot_0,
+    hot_1,
     gathered,
     far,
     terms,
@@ -88,8 +86,10 @@
     load_sem,
     send_a,
     recv_a,
+    pass_a,
     send_b,
     recv_b,
+    pass_b,
     send_t,
     recv_t,
     send_m,
@@ -101,6 +101,7 @@
     me = lax.axis_index("wide") * 2 + lax.axis_index("narrow")
     member = lax.rem(me, 4)
     group = lax.div(me, 4)
+    core = lax.rem(lax.div(me, 2), 2)
 
     def place(position):
         return (lax.div(position, 2), lax.rem(position, 2))
@@ -134,9 +135,9 @@
         (sources_0, s0),
         (couple_3, c3),
         (couple_4, c4),
-        (couple_0, c0),
-        (couple_1, c1),
-        (couple_2, c2),
+        (couple_0, couples.at[pl.ds(0, 1792)]),
+        (couple_1, couples.at[pl.ds(1792, 448)]),
+        (couple_2, couples.at[pl.ds(2240, 112)]),
     ]
     copies = [
         pltpu.make_async_copy(src, dst, load_sem.at[n]) for n, (src, dst) in enumerate(loads)
@@ -155,28 +156,84 @@
     lax.fori_loop(0, 8, build_perm, 0)
 
     copies[0].wait()
-    win_a[REACH] = jnp.dot(
-        mom[...].astype(BF16), perm[...], preferred_element_type=F32
-    ).astype(BF16)
+    own = jnp.dot(mom[...].astype(BF16), perm[...], preferred_element_type=F32).astype(BF16)
+    for h in range(PIECES):
+        win_a[h, REACH] = own[:, h * PART : (h + 1) * PART]
 
     pl.semaphore_wait(barrier, len(offsets) + tops - 3)
 
-    def exchange(window, send, recv):
-        return [
-            pltpu.make_async_remote_copy(
+    def when(condition, act):
+        if condition is None:
+            act()
+        else:
+            pl.when(condition)(act)
+
+    def direct(window, send, recv):
+        result = []
+        for n, o in enumerate(offsets):
+            target = shifted(o)
+            target_core = lax.rem(lax.div(target, 2), 2)
+            condition = None if o == -1 else target_core == (0 if o > 0 else 1)
+            copy = pltpu.make_async_remote_copy(
                 src_ref=window.at[REACH],
                 dst_ref=window.at[REACH - o],
                 send_sem=send.at[n],
                 recv_sem=recv.at[REACH - o],
-                device_id=place(shifted(o)),
+                device_id=place(target),
                 device_id_type=MESH,
             )
-            for n, o in enumerate(offsets)
-        ]
-
-    sends_a = exchange(win_a, send_a, recv_a)
-    for copy in sends_a:
-        copy.start()
+            result.append((condition, copy))
+        return result
+
+    def passes(window, send, recv, slots):
+        result = []
+        for which, by in ((0, -2), (1, 2)):
+            for slot in slots[which]:
+                copy = pltpu.make_async_remote_copy(
+                    src_ref=window.at[slot],
+                    dst_ref=window.at[slot + by],
+                    send_sem=send.at[slot],
+                    recv_sem=recv.at[slot + by],
+                    device_id=place(shifted(-by)),
+                    device_id_type=MESH,
+                )
+                result.append((core == which, copy))
+        return result
+
+    def own_rows(window, send, recv):
+        return passes(window, send, recv, ([REACH], [REACH]))
+
+    def shared_rows(window, send, recv):
+        return passes(window, send, recv, ([2, 3, 5], [5, 6]))
+
+    def start(copies):
+        for condition, copy in copies:
+            when(condition, copy.start)
+
+    def sent(copies):
+        for condition, copy in copies:
+            when(condition, copy.wait_send)
+
+    def arrived(window, recv, slots):
+        for which in (0, 1):
+            for slot in slots[which]:
+                copy = pltpu.make_async_copy(window.at[slot], window.at[slot], recv.at[slot])
+                when(core == which, copy.wait)
+
+    def arrived_direct(window, recv):
+        arrived(window, recv, ([0, 1, 2, 3, 5], [5, 6, 7, 8]))
+
+    def arrived_passed(window, recv):
+        arrived(window, recv, ([6, 7, 8], [0, 1, 2, 3]))
+
+    all_sends = []
+    for h in range(PIECES):
+        for copies_h in (
+            direct(win_a.at[h], send_a.at[h], recv_a.at[h]),
+            own_rows(win_a.at[h], pass_a.at[h], recv_a.at[h]),
+        ):
+            start(copies_h)
+            all_sends += copies_h
 
     for n in range(1, 5):
         copies[n].wait()
@@ -269,9 +326,9 @@
         axis=0,
     ).astype(BF16)
     win_b[REACH] = jnp.dot(natural, perm[...], preferred_element_type=F32).astype(BF16)
-    sends_b = exchange(win_b, send_b, recv_b)
-    for copy in sends_b:
-        copy.start()
+    for copies_b in (direct(win_b, send_b, recv_b), own_rows(win_b, pass_b, recv_b)):
+        start(copies_b)
+        all_sends += copies_b
 
     copies[5].wait()
     first = me - REACH
@@ -287,10 +344,9 @@
     lines[19:20, :28] = (sources_3[...].reshape(1, 28) - first) * 32 + 20
     lines[20:21, :7] = (sources_4[...].reshape(1, 7) - group) & (tops - 1)
     columns = lines[...].T
-    for j in range(21):
-        index[j * LANES : (j + 1) * LANES, :] = jnp.broadcast_to(
-            columns[:, j : j + 1], (LANES, LANES)
-        )
+    places = [j * LANES for j in range(18)] + [2240, 2352, 2560]
+    for j, row in enumerate(places):
+        index[row : row + LANES, :] = jnp.broadcast_to(columns[:, j : j + 1], (LANES, LANES))
 
     slot = lax.broadcasted_iota(jnp.int32, (SUPER, LANES), 0)
 
@@ -311,11 +367,36 @@
 
     drop_level(0, counts_0, 16)
     drop_level(1792, counts_1, 4)
-    drop_level(2304, counts_2, 1)
-    few = lax.broadcasted_iota(jnp.int32, (32, LANES), 0)
-    index[2432:2464, :] = jnp.where(few < counts_3[0], index[2432:2464, :], -1)
+    drop_level(2240, counts_2, 1)
+    few = lax.broadcasted_iota(jnp.int32, (48, LANES), 0)
+    index[2352:2400, :] = jnp.where(few < counts_3[0], index[2352:2400, :], -1)
     left = jnp.minimum(counts_4[group] - member * 7, 7)
-    index[2560:2592, :] = jnp.where(few < left, index[2560:2592, :], -1)
+    index[2560:2576, :] = jnp.where(few[:16] < left, index[2560:2576, :], -1)
+
+    def one_hot(from_row, count, width):
+        place_of = index[pl.ds(from_row, count), :]
+        lane = lax.broadcasted_iota(jnp.int32, (count, LANES), 1)
+        hot = [
+            jnp.where(place_of == lane + first_lane, 1.0, 0.0).astype(BF16)[
+                :, : min(LANES, width - first_lane)
+            ]
+            for first_lane in range(0, width, LANES)
+        ]
+        return jnp.concatenate(hot, axis=1) if len(hot) > 1 else hot[0]
+
+    def mark_0(n, carry):
+        row = pl.multiple_of(n * LANES, LANES)
+        hot_0[pl.ds(row, LANES), :] = one_hot(row, LANES, WINDOW * 64)
+        return carry
+
+    lax.fori_loop(0, 14, mark_0, 0)
+
+    def mark_1(n, carry):
+        row = pl.multiple_of(n * 304, 16)
+        hot_1[pl.ds(row, 304), :] = one_hot(pl.multiple_of(1792 + row, 16), 304, WINDOW * 32)
+        return carry
+
+    lax.fori_loop(0, 2, mark_1, 0)
 
     for copy in sends_t:
         copy.wait_recv()
@@ -337,33 +418,14 @@
 
     lax.fori_loop(1, tops, send_top, 0)
 
-    def picked(start, count, sources, width):
-        place_of = index[pl.ds(start, count), :]
-        lane = lax.broadcasted_iota(jnp.int32, (count, LANES), 1)
-        hot = [
-            jnp.where(place_of == lane + first_lane, 1.0, 0.0).astype(BF16)[
-                :, : min(LANES, width - first_lane)
-            ]
-            for first_lane in range(0, width, LANES)
-        ]
-        hot = jnp.concatenate(hot, axis=1) if len(hot) > 1 else hot[0]
-        return jnp.dot(hot, sources, preferred_element_type=F32).astype(BF16)
-
-    def gather(start, to, count, window, width):
-        for piece in range(0, WIDTH, 256):
-            sources = window[:, :, piece : piece + 256].reshape(width, 256)
-            gathered[pl.ds(to, count), piece : piece + 256] = picked(
-                start, count, sources, width
-            )
-
-    def turned(rows):
+    def turned_few(rows):
         stack = jnp.concatenate(
             [rows[:, i * LANES : (i + 1) * LANES] for i in range(8)], axis=0
         )
         across = stack.T
         return jnp.concatenate([across[32 * m : 32 * m + 32] for m in range(4)], axis=1)
 
-    def stacked(rows):
+    def stacked_few(rows):
         return jnp.concatenate(
             [
                 rows[:, (4 * i + m) * LANES : (4 * i + m + 1) * LANES]
@@ -373,19 +435,44 @@
             axis=0,
         )
 
+    def turned(rows):
+        stack = jnp.concatenate(
+            [rows[:, i * LANES : (i + 1) * LANES] for i in range(4)], axis=0
+        )
+        across = stack.T
+        return jnp.concatenate([across[32 * m : 32 * m + 32] for m in range(4)], axis=1)
+
+    def stacked(rows):
+        return jnp.concatenate(
+            [
+                rows[:, (4 * i + m) * LANES : (4 * i + m + 1) * LANES]
+                for m in range(4)
+                for i in range(4)
+            ],
+            axis=0,
+        )
+
     def box_tile(value):
         a, b, c, d = (value[8 * n : 8 * n + 8] for n in range(4))
         return jnp.where(low, a, d) + swap_halves(jnp.where(low, b, c))
 
-    def far_super(rows_from, couple, couple_from, far_from):
-        totals = [None] * 4
-        lane_slot = lax.broadcasted_iota(jnp.int32, (32, 512), 1) % 16
-        for g in range(GROUPS):
-            left = turned(gathered[pl.ds(rows_from + 16 * g, 16), :])
-            right = stacked(couple[pl.ds(couple_from + 16 * g, 16), :])
-            boxes = TOUCH[g]
-            if len(boxes) == 2:
-                border = boxes[1] * LIST - 16 * g
+    half = BLOCK // PIECES
+
+    def far_part(h, rows_from, couple_from, far_from, groups, boxes):
+        totals = [None] * boxes
+        lane_slot = lax.broadcasted_iota(jnp.int32, (32, 512), 1) % GROUP
+        for g in range(groups):
+            left = turned(gathered[pl.ds(rows_from + GROUP * g, GROUP), :])
+            right = stacked(
+                couples[pl.ds(couple_from + GROUP * g, GROUP), h * half : (h + 1) * half]
+            )
+            touched = [
+                b
+                for b in range(boxes)
+                if b * LIST < GROUP * (g + 1) and (b + 1) * LIST > GROUP * g
+            ]
+            if len(touched) == 2:
+                border = touched[1] * LIST - GROUP * g
                 zero = jnp.zeros_like(left)
                 left = jnp.concatenate(
                     [
@@ -395,36 +482,57 @@
                     axis=0,
                 )
             value = jnp.dot(left, right, preferred_element_type=F32)
-            for n, b in enumerate(boxes):
+            for n, b in enumerate(touched):
                 part = value[32 * n : 32 * n + 32]
                 totals[b] = part if totals[b] is None else totals[b] + part
-        for b in range(4):
-            far[pl.ds(far_from + 8 * b, 8), :] = box_tile(totals[b])
-
-    for copy in sends_a:
-        copy.wait_recv()
-
-    def gather_0(n, carry):
-        start = pl.multiple_of(n * 448, 448)
-        gather(start, start, 448, win_a, WINDOW * 64)
-        return carry
-
-    lax.fori_loop(0, 4, gather_0, 0)
-    copies[8].wait()
-
-    def far_0(n, carry):
-        start = pl.multiple_of(n * SUPER, SUPER)
-        far_super(start, c0, start, pl.multiple_of(n * 32, 32))
-        return carry
-
-    lax.fori_loop(0, 16, far_0, 0)
-
+        for b in range(boxes):
+            rows = pl.ds(far_from + 8 * b, 8)
+            if h == 0:
+                far[rows, :] = box_tile(totals[b])
+            else:
+                far[rows, :] += box_tile(totals[b])
+
+    def gather_0(h):
+        sources = win_a[h].reshape(WINDOW * 64, PART)
+
+        def step(n, carry):
+            rows = pl.ds(pl.multiple_of(n * 448, 448), 448)
+            gathered[rows, :] = jnp.dot(
+                hot_0[rows, :], sources, preferred_element_type=F32
+            ).astype(BF16)
+            return carry
+
+        lax.fori_loop(0, 4, step, 0)
+
+    def far_0(h, first, last):
+        def step(n, carry):
+            row = pl.multiple_of(n * WIDE, WIDE)
+            far_part(h, row, row, pl.multiple_of(n * 64, 64), 7, 8)
+            return carry
+
+        lax.fori_loop(first, last, step, 0)
+
+    arrived_direct(win_a.at[0], recv_a.at[0])
+    shared = shared_rows(win_a.at[0], pass_a.at[0], recv_a.at[0])
+    start(shared)
+    all_sends += shared
     copies[6].wait()
     copies[7].wait()
     pad4[...] = jnp.zeros_like(pad4)
     pad4[0:7, :] = c4[...].astype(F32)
     pad3[...] = jnp.zeros_like(pad3)
     pad3[0:28, :] = c3[...].astype(F32)
+    couples[2352:2384, :] = pad3[...].astype(BF16)
+    couples[2384:2400, :] = jnp.zeros((16, BLOCK), BF16)
+    arrived_passed(win_a.at[0], recv_a.at[0])
+    gather_0(0)
+    copies[8].wait()
+    far_0(0, 0, 4)
+    arrived_direct(win_a.at[1], recv_a.at[1])
+    shared = shared_rows(win_a.at[1], pass_a.at[1], recv_a.at[1])
+    start(shared)
+    all_sends += shared
+    far_0(0, 4, 8)
 
     def all_top(n):
         return pltpu.make_async_copy(
@@ -447,35 +555,40 @@
         axis=0,
     ).astype(BF16)
     top_rows = jnp.dot(natural, perm[...], preferred_element_type=F32).astype(BF16)
-    left = turned(picked(2560, 16, top_rows, count))
-    right = stacked(pad4[...].astype(BF16))
+    rows = jnp.dot(one_hot(2560, 16, count), top_rows, preferred_element_type=F32)
+    left = turned_few(rows.astype(BF16))
+    right = stacked_few(pad4[...].astype(BF16))
     parts[0] = box_tile(jnp.dot(left, right, preferred_element_type=F32))
     sends_f = to_mates(parts, send_f, recv_f)
     for copy in sends_f:
         copy.start()
 
-    for copy in sends_b:
-        copy.wait_recv()
+    arrived_passed(win_a.at[1], recv_a.at[1])
+    gather_0(1)
+    far_0(1, 0, 4)
+    arrived_direct(win_b, recv_b)
+    shared = shared_rows(win_b, pass_b, recv_b)
+    start(shared)
+    all_sends += shared
+    far_0(1, 4, 8)
+
+    arrived_passed(win_b, recv_b)
     copies[9].wait()
     copies[10].wait()
-    gather(1792, 0, 448, win_b, WINDOW * 32)
-    gather(2304, 448, SUPER, win_b, WINDOW * 32)
-    gather(2432, 560, 32, win_b, WINDOW * 32)
-
-    def far_1(n, carry):
-        start = pl.multiple_of(n * SUPER, SUPER)
-        far_super(start, c1, start, pl.multiple_of(512 + n * 32, 32))
-        return carry
-
-    lax.fori_loop(0, 4, far_1, 0)
-    far_super(448, c2, 0, 640)
-    total = None
-    for g in range(2):
-        left = turned(gathered[560 + 16 * g : 576 + 16 * g, :])
-        right = stacked(pad3[16 * g : 16 * g + 16, :].astype(BF16))
-        value = jnp.dot(left, right, preferred_element_type=F32)
-        total = value if total is None else total + value
-    far_3 = box_tile(total)
+    for h in range(PIECES):
+        gathered[0:608, :] = jnp.dot(
+            hot_1[...],
+            win_b[:, :, h * PART : (h + 1) * PART].reshape(WINDOW * 32, PART),
+            preferred_element_type=F32,
+        ).astype(BF16)
+
+        def far_1(n, carry):
+            row = pl.multiple_of(n * WIDE, WIDE)
+            far_part(h, row, 1792 + row, 512 + pl.multiple_of(n * 64, 64), 7, 8)
+            return carry
+
+        lax.fori_loop(0, 2, far_1, 0)
+        far_part(h, 448, 2240, 640, 5, 5)
 
     def lowered(parent, base, boxes):
         rows = jnp.concatenate(
@@ -508,7 +621,7 @@
         preferred_element_type=F32,
     )
     product = jnp.concatenate([product, jnp.zeros_like(product)], axis=1)
-    field_3 = far_3 + jnp.where(low, product[:8], swap_halves(product[8:]))
+    field_3 = far[672:680, :] + jnp.where(low, product[:8], swap_halves(product[8:]))
     down = lowered(field_3, 80, 4)
     field_2 = [far[640 + 8 * c : 648 + 8 * c, :] + down[c] for c in range(4)]
     field_1 = []
@@ -529,8 +642,9 @@
             row = (big * 8 + j) * 8
             out[big * 8 : big * 8 + 8, j * LANES : (j + 1) * LANES] = tiles[row : row + 8, :]
 
-    for copy in sends_a + sends_b + sends_t + sends_f:
+    for copy in sends_t + sends_f:
         copy.wait_send()
+    sent(all_sends)
     all_top(send_m).wait()
 
 
@@ -557,9 +671,7 @@
                 vmem((16, BLOCK), BF16),
                 vmem((4, BLOCK), BF16),
                 vmem((1, BLOCK), BF16),
-                vmem((1792, BLOCK), BF16),
-                vmem((448, BLOCK), BF16),
-                vmem((112, BLOCK), BF16),
+                vmem((2400, BLOCK), BF16),
                 vmem((28, BLOCK), BF16),
                 vmem((7, BLOCK), BF16),
                 vmem((1792,), jnp.int32),
@@ -568,21 +680,25 @@
                 vmem((512, LANES), F32),
                 vmem((256, LANES), F32),
                 vmem((WIDTH, WIDTH), BF16),
-                vmem((WINDOW, 64, WIDTH), BF16),
+                vmem((PIECES, WINDOW, 64, PART), BF16),
                 vmem((WINDOW, 32, WIDTH), BF16),
                 vmem((85 * RANK, LANES), F32),
                 vmem((85 * RANK, LANES), BF16),
                 vmem((32, LANES), jnp.int32),
                 vmem((21 * LANES, LANES), jnp.int32),
-                vmem((1792, WIDTH), BF16),
-                vmem((84 * 8, LANES), F32),
+                vmem((1792, WINDOW * 64), BF16),
+                vmem((608, WINDOW * 32), BF16),
+                vmem((1792, PART), BF16),
+                vmem((85 * 8, LANES), F32),
                 vmem((4, 8, LANES), F32),
                 vmem((tops, 8, LANES), F32),
                 vmem((4, 8, LANES), F32),
                 dma((11,)),
+                dma((PIECES, 2 * REACH)),
+                dma((PIECES, WINDOW)),
+                dma((PIECES, WINDOW)),
                 dma((2 * REACH,)),
                 dma((WINDOW,)),
-                dma((2 * REACH,)),
                 dma((WINDOW,)),
                 dma((4,)),
                 dma((4,)),

time: 47.4 us -> 44.4 us (0.937)
  Pallas kernels: 44.9 us -> 41.9 us
    pallas_call x1, Pallas kernels: 44.9 us -> 41.9 us  [body(): pl.pallas_call(functools.partial(kernel, devices), out_shape=jax.ShapeDty...]
where the time goes in v2:
time: 44.4 us; the launch traced here: 44.2 us
  Pallas kernels  41.9 us (94%)
  local copies, waits for them, and re-layouts  1.67 us (4%)
  between operations  0.66 us (1%)
    pallas_call x1, Pallas kernels, body(): pl.pallas_call(functools.partial(kernel, devices), out_shape=jax.ShapeDty...  41.9 us
    unnamed x1, local copies, waits for them, and re-layouts  1.67 us

profile of v2, /device:TPU:1, one launch (start us, length us, event | category | flops | bytes accessed | tf_op | source)
XLA Modules:
  0.0 44.2 jit_solution(12823367379457987345)
XLA Ops:
  0.7 41.9 %shard_map.190 = f32[64,1024]{1,0:T(8,128)} custom-call(f32[64,1024]{1,0:T(8,128)} %moments.1, bf16[64,4096]{1,0:T(8,128)(2,1)} %up_0.1, bf16[16,4096]{1,0:T(8,128)(2,1)} %up_1.1, bf16[4,4096]{1,0:T(4,128)(2,1)} %up_2.1, bf16[1,4096]{1,0:T(2,128)(2,1)} %up_3.1, bf16[1792,4096]{1,0:T(8,128)(2,1)} %couple_0.1, bf16[448,4096]{1,0:T(8,128)(2,1)} %couple_1.1, ...), custom_call_target="tpu_custom_call" | custom-call | tf_op jit(solution)/shard_map/pallas_call | solution.py:663
  42.5 1.7 %copy.23 = f32[64,1024]{1,0:T(8,128)} copy(f32[64,1024]{1,0:T(8,128)} %shard_map.190) | data formatting | bytes 524288

commit v3 on v2

--- a/solution.py
+++ b/solution.py
@@ -35,6 +35,7 @@
 
 def kernel(
     devices,
+    planes,
     moments,
     up_0,
     up_1,
@@ -72,7 +73,9 @@
     perm,
     win_a,
     win_b,
-    up_f,
+    few_up,
+    by_pair,
+    by_row,
     up_b,
     lines,
     index,
@@ -82,7 +85,7 @@
     far,
     terms,
     top,
-    parts,
+    slots_4,
     load_sem,
     send_a,
     recv_a,
@@ -92,39 +95,70 @@
     pass_b,
     send_t,
     recv_t,
-    send_m,
-    recv_m,
-    send_f,
-    recv_f,
+    send_z,
+    recv_z,
+    send_y,
+    recv_y,
+    send_s,
+    recv_s,
+    send_c,
+    recv_c,
 ):
-    tops = devices // 4
+    rows = devices // 8 // planes
     me = lax.axis_index("wide") * 2 + lax.axis_index("narrow")
     member = lax.rem(me, 4)
     group = lax.div(me, 4)
     core = lax.rem(lax.div(me, 2), 2)
+    seat = lax.rem(me, 8)
+    my_row = lax.div(me, 8)
+    z, y = lax.rem(my_row, rows), lax.div(my_row, rows)
+    opposite = me + 1 - 2 * lax.rem(me, 2)
+    sibling = me + 2 - 4 * core
 
     def place(position):
         return (lax.div(position, 2), lax.rem(position, 2))
 
-    def shifted(by):
-        return lax.rem(me + by + devices, devices)
-
     def mate(v):
         return group * 4 + lax.rem(member + v, 4)
 
+    def row_mate(v):
+        return my_row * 8 + lax.rem(seat + v, 8)
+
+    def along_z(k):
+        return (y * rows + lax.rem(z + k, rows)) * 8 + seat
+
+    def along_y(k):
+        return (lax.rem(y + k, planes) * rows + z) * 8 + seat
+
+    def exists(o):
+        return jnp.logical_and(me + o >= 0, me + o < devices)
+
     offsets = [o for o in range(-REACH, REACH + 1) if o != 0]
 
+    for o in offsets:
+
+        @pl.when(jnp.logical_not(exists(o)))
+        def _():
+            for h in range(PIECES):
+                win_a[h, REACH + o] = jnp.zeros((64, PART), BF16)
+            win_b[REACH + o] = jnp.zeros((32, WIDTH), BF16)
+
     barrier = pltpu.get_barrier_semaphore()
-    for o in offsets:
-        pl.semaphore_signal(barrier, inc=1, device_id=place(shifted(o)), device_id_type=MESH)
-
-    def greet(u, carry):
-        pl.semaphore_signal(
-            barrier, inc=1, device_id=place(shifted(4 * u)), device_id_type=MESH
-        )
-        return carry
-
-    lax.fori_loop(2, tops - 1, greet, 0)
+
+    def greet(position):
+        pl.semaphore_signal(barrier, inc=1, device_id=place(position), device_id_type=MESH)
+
+    greeted = jnp.int32(rows - 1 + planes - 1)
+    for o in offsets + [-7, -6, -5, 5, 6, 7]:
+        known = exists(o)
+        if abs(o) > REACH:
+            known = jnp.logical_and(seat + o >= 0, seat + o < 8)
+        pl.when(known)(functools.partial(greet, me + o))
+        greeted = greeted + known.astype(jnp.int32)
+    for k in range(1, rows):
+        greet(along_z(k))
+    for k in range(1, planes):
+        greet(along_y(k))
 
     loads = [
         (moments, mom),
@@ -134,7 +168,7 @@
         (up_3, u3),
         (sources_0, s0),
         (couple_3, c3),
-        (couple_4, c4),
+        (couple_4, c4.at[member]),
         (couple_0, couples.at[pl.ds(0, 1792)]),
         (couple_1, couples.at[pl.ds(1792, 448)]),
         (couple_2, couples.at[pl.ds(2240, 112)]),
@@ -155,25 +189,31 @@
 
     lax.fori_loop(0, 8, build_perm, 0)
 
+    a = lax.broadcasted_iota(jnp.int32, (512, 512), 0)
+    b = lax.broadcasted_iota(jnp.int32, (512, 512), 1)
+    by_pair[...] = jnp.where(b == (a % 32) * 16 + a // 32, 1.0, 0.0).astype(BF16)
+    a = lax.broadcasted_iota(jnp.int32, (256, 256), 0)
+    b = lax.broadcasted_iota(jnp.int32, (256, 256), 1)
+    by_row[...] = jnp.where(b == (a % 2) * 128 + a // 2, 1.0, 0.0).astype(BF16)
+
     copies[0].wait()
     own = jnp.dot(mom[...].astype(BF16), perm[...], preferred_element_type=F32).astype(BF16)
     for h in range(PIECES):
         win_a[h, REACH] = own[:, h * PART : (h + 1) * PART]
 
-    pl.semaphore_wait(barrier, len(offsets) + tops - 3)
+    pl.semaphore_wait(barrier, greeted)
 
     def when(condition, act):
-        if condition is None:
-            act()
-        else:
-            pl.when(condition)(act)
+        pl.when(condition)(act)
 
     def direct(window, send, recv):
         result = []
         for n, o in enumerate(offsets):
-            target = shifted(o)
-            target_core = lax.rem(lax.div(target, 2), 2)
-            condition = None if o == -1 else target_core == (0 if o > 0 else 1)
+            target = me + o
+            target_core = lax.rem(lax.div(target + 4, 2), 2)
+            condition = exists(o)
+            if o != -1:
+                condition = jnp.logical_and(condition, target_core == (0 if o > 0 else 1))
             copy = pltpu.make_async_remote_copy(
                 src_ref=window.at[REACH],
                 dst_ref=window.at[REACH - o],
@@ -194,10 +234,10 @@
                     dst_ref=window.at[slot + by],
                     send_sem=send.at[slot],
                     recv_sem=recv.at[slot + by],
-                    device_id=place(shifted(-by)),
+                    device_id=place(me - by),
                     device_id_type=MESH,
                 )
-                result.append((core == which, copy))
+                result.append((jnp.logical_and(core == which, exists(slot - REACH)), copy))
         return result
 
     def own_rows(window, send, recv):
@@ -218,7 +258,7 @@
         for which in (0, 1):
             for slot in slots[which]:
                 copy = pltpu.make_async_copy(window.at[slot], window.at[slot], recv.at[slot])
-                when(core == which, copy.wait)
+                when(jnp.logical_and(core == which, exists(slot - REACH)), copy.wait)
 
     def arrived_direct(window, recv):
         arrived(window, recv, ([0, 1, 2, 3, 5], [5, 6, 7, 8]))
@@ -226,43 +266,50 @@
     def arrived_passed(window, recv):
         arrived(window, recv, ([6, 7, 8], [0, 1, 2, 3]))
 
-    all_sends = []
-    for h in range(PIECES):
-        for copies_h in (
-            direct(win_a.at[h], send_a.at[h], recv_a.at[h]),
-            own_rows(win_a.at[h], pass_a.at[h], recv_a.at[h]),
-        ):
-            start(copies_h)
-            all_sends += copies_h
+    def send_part(h):
+        result = direct(win_a.at[h], send_a.at[h], recv_a.at[h])
+        result += own_rows(win_a.at[h], pass_a.at[h], recv_a.at[h])
+        start(result)
+        return result
+
+    all_sends = send_part(0)
+
+    def whole(ref, to, send_sem, recv_sem):
+        return pltpu.make_async_remote_copy(
+            src_ref=ref,
+            dst_ref=ref,
+            send_sem=send_sem,
+            recv_sem=recv_sem,
+            device_id=place(to),
+            device_id_type=MESH,
+        )
 
     for n in range(1, 5):
         copies[n].wait()
-    bases = [0, 64, 80, 84]
-
-    def spread(m, carry):
-        lane = pl.ds(pl.multiple_of(m * LANES, LANES), LANES)
-        for source, base, boxes in ((u0, 0, 64), (u1, 64, 16), (u2, 80, 4), (u3, 84, 1)):
-            block = source[:, lane].astype(F32)
-            other = swap_halves(block)
-            step = min(boxes, 8)
-            for first in range(0, boxes, step):
-                for kp, value in ((0, block), (1, other)):
-                    start = (base + first) * RANK + 2 * m + kp
-                    piece = value[first : first + step]
-                    if step > 1:
-                        up_f[pl.ds(start, step, stride=RANK), :] = piece
-                    else:
-                        up_f[pl.ds(start, 1), :] = piece
-        return carry
-
-    lax.fori_loop(0, 32, spread, 0)
-
-    def narrowed(n, carry):
-        rows = pl.ds(pl.multiple_of(n * 320, 320), 320)
-        up_b[rows, :] = up_f[rows, :].astype(BF16)
-        return carry
-
-    lax.fori_loop(0, 17, narrowed, 0)
+    few_up[...] = jnp.zeros_like(few_up)
+    few_up[0:4, :] = u2[...].astype(F32)
+    few_up[4:5, :] = u3[...].astype(F32)
+    blocks = [u0[16 * n : 16 * n + 16, :] for n in range(4)]
+    blocks += [u1[...], few_up[...].astype(BF16)]
+    columns = jnp.concatenate(
+        [
+            jnp.concatenate([block[:, m * LANES : (m + 1) * LANES] for m in range(32)], axis=0)
+            for block in blocks
+        ],
+        axis=1,
+    )
+    by_box = jnp.dot(by_pair[...], columns, preferred_element_type=F32)
+    for n in range(6):
+        quads = []
+        for p in range(4 if n < 5 else 2):
+            one = by_box[128 * p : 128 * p + 128, n * LANES : (n + 1) * LANES]
+            quads.append(jnp.concatenate([one, swap_halves(one)], axis=0).astype(BF16))
+        upright = jnp.dot(
+            by_row[...], jnp.concatenate(quads, axis=1), preferred_element_type=F32
+        ).astype(BF16)
+        for p in range(len(quads)):
+            base = (4 * n + p) * 256
+            up_b[base : base + 256, :] = upright[:, p * LANES : (p + 1) * LANES]
 
     for big in range(8):
         for j in range(8):
@@ -294,24 +341,15 @@
     level_3 = lifted(level_2, 80)
     alone = jnp.concatenate([level_3, swap_halves(level_3)], axis=0)[:, :RANK].astype(BF16)
     product = jnp.dot(alone, up_b[84 * RANK : 85 * RANK, :], preferred_element_type=F32)
-    terms[0] = jnp.where(low, product[:8], swap_halves(product[8:]))
-
-    def to_mates(buffer, send, recv):
-        return [
-            pltpu.make_async_remote_copy(
-                src_ref=buffer.at[0],
-                dst_ref=buffer.at[4 - v],
-                send_sem=send.at[v],
-                recv_sem=recv.at[4 - v],
-                device_id=place(mate(v)),
-                device_id_type=MESH,
-            )
-            for v in (1, 2, 3)
-        ]
-
-    sends_t = to_mates(terms, send_t, recv_t)
+    terms[seat] = jnp.where(low, product[:8], swap_halves(product[8:]))
+
+    sends_t = [
+        whole(terms.at[seat], row_mate(v), send_t.at[v], recv_t.at[8 - v]) for v in range(1, 8)
+    ]
     for copy in sends_t:
         copy.start()
+
+    all_sends += send_part(1)
 
     rows_b[...] = jnp.zeros_like(rows_b)
     for row, value in enumerate(level_1 + level_2 + [level_3]):
@@ -326,9 +364,6 @@
         axis=0,
     ).astype(BF16)
     win_b[REACH] = jnp.dot(natural, perm[...], preferred_element_type=F32).astype(BF16)
-    for copies_b in (direct(win_b, send_b, recv_b), own_rows(win_b, pass_b, recv_b)):
-        start(copies_b)
-        all_sends += copies_b
 
     copies[5].wait()
     first = me - REACH
@@ -342,9 +377,8 @@
     local = sources_2[...].reshape(1, 112) - first * 4
     lines[18:19, :112] = (local >> 2) * 32 + 16 + (local & 3)
     lines[19:20, :28] = (sources_3[...].reshape(1, 28) - first) * 32 + 20
-    lines[20:21, :7] = (sources_4[...].reshape(1, 7) - group) & (tops - 1)
     columns = lines[...].T
-    places = [j * LANES for j in range(18)] + [2240, 2352, 2560]
+    places = [j * LANES for j in range(18)] + [2240, 2352]
     for j, row in enumerate(places):
         index[row : row + LANES, :] = jnp.broadcast_to(columns[:, j : j + 1], (LANES, LANES))
 
@@ -370,8 +404,6 @@
     drop_level(2240, counts_2, 1)
     few = lax.broadcasted_iota(jnp.int32, (48, LANES), 0)
     index[2352:2400, :] = jnp.where(few < counts_3[0], index[2352:2400, :], -1)
-    left = jnp.minimum(counts_4[group] - member * 7, 7)
-    index[2560:2576, :] = jnp.where(few[:16] < left, index[2560:2576, :], -1)
 
     def one_hot(from_row, count, width):
         place_of = index[pl.ds(from_row, count), :]
@@ -398,42 +430,34 @@
 
     lax.fori_loop(0, 2, mark_1, 0)
 
-    for copy in sends_t:
-        copy.wait_recv()
-    top[0] = (terms[0] + terms[1]) + (terms[2] + terms[3])
-
-    def to_top(u):
-        return pltpu.make_async_remote_copy(
-            src_ref=top.at[0],
-            dst_ref=top.at[tops - u],
-            send_sem=send_m,
-            recv_sem=recv_m,
-            device_id=place(shifted(4 * u)),
-            device_id_type=MESH,
-        )
-
-    def send_top(u, carry):
-        to_top(u).start()
-        return carry
-
-    lax.fori_loop(1, tops, send_top, 0)
-
-    def turned_few(rows):
-        stack = jnp.concatenate(
-            [rows[:, i * LANES : (i + 1) * LANES] for i in range(8)], axis=0
-        )
-        across = stack.T
-        return jnp.concatenate([across[32 * m : 32 * m + 32] for m in range(4)], axis=1)
-
-    def stacked_few(rows):
-        return jnp.concatenate(
-            [
-                rows[:, (4 * i + m) * LANES : (4 * i + m + 1) * LANES]
-                for m in range(4)
-                for i in range(8)
-            ],
-            axis=0,
-        )
+    for v in range(1, 8):
+        pltpu.make_async_copy(terms.at[0], terms.at[0], recv_t.at[v]).wait()
+    for n in range(2):
+        four = [terms[4 * n + c] for c in range(4)]
+        top[y, z, n] = (four[0] + four[1]) + (four[2] + four[3])
+    sends_z = [
+        whole(top.at[y, z], along_z(k), send_z.at[k], recv_z.at[rows - k])
+        for k in range(1, rows)
+    ]
+    for copy in sends_z:
+        copy.start()
+    slots_4[member] = jnp.zeros((8, LANES), jnp.int32)
+    slots_4[member, 0:1, :7] = sources_4[...].reshape(1, 7)
+    copies[7].wait()
+    sends_s = [
+        whole(slots_4.at[member], mate(v), send_s.at[v], recv_s.at[4 - v]) for v in (1, 2, 3)
+    ]
+    sends_c = [
+        whole(c4.at[member], opposite, send_c.at[0], recv_c.at[0]),
+        whole(c4.at[member], sibling, send_c.at[1], recv_c.at[1]),
+    ]
+    for copy in sends_s + sends_c:
+        copy.start()
+
+
+    for copies_b in (direct(win_b, send_b, recv_b), own_rows(win_b, pass_b, recv_b)):
+        start(copies_b)
+        all_sends += copies_b
 
     def turned(rows):
         stack = jnp.concatenate(
@@ -496,13 +520,13 @@
         sources = win_a[h].reshape(WINDOW * 64, PART)
 
         def step(n, carry):
-            rows = pl.ds(pl.multiple_of(n * 448, 448), 448)
+            rows = pl.ds(pl.multiple_of(n * 896, 896), 896)
             gathered[rows, :] = jnp.dot(
                 hot_0[rows, :], sources, preferred_element_type=F32
             ).astype(BF16)
             return carry
 
-        lax.fori_loop(0, 4, step, 0)
+        lax.fori_loop(0, 2, step, 0)
 
     def far_0(h, first, last):
         def step(n, carry):
@@ -510,16 +534,13 @@
             far_part(h, row, row, pl.multiple_of(n * 64, 64), 7, 8)
             return carry
 
-        lax.fori_loop(first, last, step, 0)
+        lax.fori_loop(first, last, step, 0, unroll=2)
 
     arrived_direct(win_a.at[0], recv_a.at[0])
     shared = shared_rows(win_a.at[0], pass_a.at[0], recv_a.at[0])
     start(shared)
     all_sends += shared
     copies[6].wait()
-    copies[7].wait()
-    pad4[...] = jnp.zeros_like(pad4)
-    pad4[0:7, :] = c4[...].astype(F32)
     pad3[...] = jnp.zeros_like(pad3)
     pad3[0:28, :] = c3[...].astype(F32)
     couples[2352:2384, :] = pad3[...].astype(BF16)
@@ -532,19 +553,70 @@
     shared = shared_rows(win_a.at[1], pass_a.at[1], recv_a.at[1])
     start(shared)
     all_sends += shared
+    for k in range(1, rows):
+        pltpu.make_async_copy(top.at[y, z], top.at[y, z], recv_z.at[k]).wait()
+    sends_y = [
+        whole(top.at[y], along_y(k), send_y.at[k], recv_y.at[planes - k])
+        for k in range(1, planes)
+    ]
+    for copy in sends_y:
+        copy.start()
+    back = member + 1 - 2 * lax.rem(member, 2)
+    pltpu.make_async_copy(c4.at[back], c4.at[back], recv_c.at[0]).wait()
+    sends_c.append(whole(c4.at[back], sibling, send_c.at[2], recv_c.at[2]))
+    sends_c[2].start()
     far_0(0, 4, 8)
 
-    def all_top(n):
-        return pltpu.make_async_copy(
-            top.at[pl.ds(1, tops - 1)], top.at[pl.ds(1, tops - 1)], n
-        )
-
-    all_top(recv_m).wait()
+    arrived_passed(win_a.at[1], recv_a.at[1])
+    gather_0(1)
+    far_0(1, 0, 4)
+    arrived_direct(win_b, recv_b)
+    shared = shared_rows(win_b, pass_b, recv_b)
+    start(shared)
+    all_sends += shared
+    far_0(1, 4, 8)
+
+    arrived_passed(win_b, recv_b)
+    copies[9].wait()
+    copies[10].wait()
+    for h in range(PIECES):
+        gathered[0:608, :] = jnp.dot(
+            hot_1[...],
+            win_b[:, :, h * PART : (h + 1) * PART].reshape(WINDOW * 32, PART),
+            preferred_element_type=F32,
+        ).astype(BF16)
+
+        def far_1(n, carry):
+            row = pl.multiple_of(n * WIDE, WIDE)
+            far_part(h, row, 1792 + row, 512 + pl.multiple_of(n * 64, 64), 7, 8)
+            return carry
+
+        lax.fori_loop(0, 2, far_1, 0)
+        far_part(h, 448, 2240, 640, 5, 5)
+
+    for k in range(1, planes):
+        pltpu.make_async_copy(top.at[y], top.at[y], recv_y.at[k]).wait()
+    for v in (1, 2, 3):
+        pltpu.make_async_copy(slots_4.at[0], slots_4.at[0], recv_s.at[v]).wait()
+    for v in (1, 2):
+        pltpu.make_async_copy(c4.at[0], c4.at[0], recv_c.at[v]).wait()
+    pad4[...] = jnp.zeros_like(pad4)
+    for n in range(4):
+        pad4[7 * n : 7 * n + 7, :] = c4[n].astype(F32)
+        lines[n : n + 1, :] = slots_4[n, 0:1, :]
+    columns = lines[...].T
+    for n in range(4):
+        index[2560 + 7 * n : 2568 + 7 * n, :] = jnp.broadcast_to(columns[:8, n : n + 1], (8, LANES))
+    few = lax.broadcasted_iota(jnp.int32, (32, LANES), 0)
+    index[2560:2592, :] = jnp.where(few < counts_4[group], index[2560:2592, :], -1)
+    tops = 2 * rows * planes
     count = max(tops, 8)
     if tops < 8:
         tiles[0:512, :] = jnp.zeros((512, LANES), F32)
-    for row in range(tops):
-        tiles[pl.ds((row // 8) * 64 + row % 8, 8, stride=8), :] = top[row]
+    for box in range(tops):
+        tiles[pl.ds((box // 8) * 64 + box % 8, 8, stride=8), :] = top[
+            box // 2 // rows, box // 2 % rows, box % 2
+        ]
     natural = jnp.concatenate(
         [
             jnp.concatenate(
@@ -555,48 +627,26 @@
         axis=0,
     ).astype(BF16)
     top_rows = jnp.dot(natural, perm[...], preferred_element_type=F32).astype(BF16)
-    rows = jnp.dot(one_hot(2560, 16, count), top_rows, preferred_element_type=F32)
-    left = turned_few(rows.astype(BF16))
-    right = stacked_few(pad4[...].astype(BF16))
-    parts[0] = box_tile(jnp.dot(left, right, preferred_element_type=F32))
-    sends_f = to_mates(parts, send_f, recv_f)
-    for copy in sends_f:
-        copy.start()
-
-    arrived_passed(win_a.at[1], recv_a.at[1])
-    gather_0(1)
-    far_0(1, 0, 4)
-    arrived_direct(win_b, recv_b)
-    shared = shared_rows(win_b, pass_b, recv_b)
-    start(shared)
-    all_sends += shared
-    far_0(1, 4, 8)
-
-    arrived_passed(win_b, recv_b)
-    copies[9].wait()
-    copies[10].wait()
-    for h in range(PIECES):
-        gathered[0:608, :] = jnp.dot(
-            hot_1[...],
-            win_b[:, :, h * PART : (h + 1) * PART].reshape(WINDOW * 32, PART),
-            preferred_element_type=F32,
-        ).astype(BF16)
-
-        def far_1(n, carry):
-            row = pl.multiple_of(n * WIDE, WIDE)
-            far_part(h, row, 1792 + row, 512 + pl.multiple_of(n * 64, 64), 7, 8)
-            return carry
-
-        lax.fori_loop(0, 2, far_1, 0)
-        far_part(h, 448, 2240, 640, 5, 5)
-
-    def lowered(parent, base, boxes):
+    rows_4 = jnp.dot(one_hot(2560, 32, count), top_rows, preferred_element_type=F32).astype(BF16)
+    blocks_4 = pad4[...].astype(BF16)
+    far_4 = box_tile(
+        sum(
+            jnp.dot(
+                turned(rows_4[:, h * PART : (h + 1) * PART]),
+                stacked(blocks_4[:, h * half : (h + 1) * half]),
+                preferred_element_type=F32,
+            )
+            for h in range(PIECES)
+        )
+    )
+
+    def lowered(parent, n, boxes):
         rows = jnp.concatenate(
             [jnp.where(low, parent, 0.0), jnp.where(low, swap_halves(parent), 0.0)], axis=0
         ).astype(BF16)
         product = lax.dot_general(
             rows,
-            up_b[base * RANK : (base + boxes) * RANK, :],
+            up_b[n * 256 : n * 256 + boxes * RANK, :],
             (((1,), (1,)), ((), ())),
             preferred_element_type=F32,
         )
@@ -608,30 +658,17 @@
             result.append(jnp.where(low, swap_halves(even), odd))
         return result
 
-    for copy in sends_f:
-        copy.wait_recv()
-    field_4 = (parts[0] + parts[1]) + (parts[2] + parts[3])
-    rows = jnp.concatenate(
-        [jnp.where(low, field_4, 0.0), jnp.where(low, swap_halves(field_4), 0.0)], axis=0
-    ).astype(BF16)
-    product = lax.dot_general(
-        rows,
-        up_b[84 * RANK : 85 * RANK, :],
-        (((1,), (1,)), ((), ())),
-        preferred_element_type=F32,
-    )
-    product = jnp.concatenate([product, jnp.zeros_like(product)], axis=1)
-    field_3 = far[672:680, :] + jnp.where(low, product[:8], swap_halves(product[8:]))
-    down = lowered(field_3, 80, 4)
+    field_3 = far[672:680, :] + lowered(far_4, 21, 2)[0]
+    down = lowered(field_3, 20, 4)
     field_2 = [far[640 + 8 * c : 648 + 8 * c, :] + down[c] for c in range(4)]
     field_1 = []
     for p in range(4):
-        down = lowered(field_2[p], 64 + 4 * p, 4)
+        down = lowered(field_2[p], 16 + p, 4)
         for c in range(4):
             row = 512 + 8 * (4 * p + c)
             field_1.append(far[row : row + 8, :] + down[c])
     for p in range(16):
-        down = lowered(field_1[p], 4 * p, 4)
+        down = lowered(field_1[p], p, 4)
         for c in range(4):
             box = 4 * p + c
             tiles[pl.ds((box // 8) * 64 + box % 8, 8, stride=8), :] = (
@@ -642,15 +679,14 @@
             row = (big * 8 + j) * 8
             out[big * 8 : big * 8 + 8, j * LANES : (j + 1) * LANES] = tiles[row : row + 8, :]
 
-    for copy in sends_t + sends_f:
+    for copy in sends_t + sends_s + sends_c + sends_z + sends_y:
         copy.wait_send()
     sent(all_sends)
-    all_top(send_m).wait()
 
 
 def solution(mesh):
     devices = mesh.shape["wide"] * mesh.shape["narrow"]
-    tops = devices // 4
+    planes = max(1, devices // 32)
     split = P(("wide", "narrow"), None)
     line = P(("wide", "narrow"))
     anywhere = pl.BlockSpec(memory_space=pl.ANY)
@@ -661,7 +697,7 @@
 
     def body(*arrays):
         return pl.pallas_call(
-            functools.partial(kernel, devices),
+            functools.partial(kernel, devices, planes),
             out_shape=jax.ShapeDtypeStruct((64, WIDTH), F32),
             in_specs=[anywhere] * 11 + [inside] * 4 + [scalars] * 5,
             out_specs=pl.BlockSpec(memory_space=pltpu.VMEM),
@@ -673,26 +709,28 @@
                 vmem((1, BLOCK), BF16),
                 vmem((2400, BLOCK), BF16),
                 vmem((28, BLOCK), BF16),
-                vmem((7, BLOCK), BF16),
+                vmem((4, 7, BLOCK), BF16),
                 vmem((1792,), jnp.int32),
                 vmem((32, BLOCK), F32),
-                vmem((16, BLOCK), F32),
+                vmem((32, BLOCK), F32),
                 vmem((512, LANES), F32),
                 vmem((256, LANES), F32),
                 vmem((WIDTH, WIDTH), BF16),
                 vmem((PIECES, WINDOW, 64, PART), BF16),
                 vmem((WINDOW, 32, WIDTH), BF16),
-                vmem((85 * RANK, LANES), F32),
-                vmem((85 * RANK, LANES), BF16),
+                vmem((16, BLOCK), F32),
+                vmem((512, 512), BF16),
+                vmem((256, 256), BF16),
+                vmem((96 * RANK, LANES), BF16),
                 vmem((32, LANES), jnp.int32),
                 vmem((21 * LANES, LANES), jnp.int32),
                 vmem((1792, WINDOW * 64), BF16),
                 vmem((608, WINDOW * 32), BF16),
                 vmem((1792, PART), BF16),
                 vmem((85 * 8, LANES), F32),
-                vmem((4, 8, LANES), F32),
-                vmem((tops, 8, LANES), F32),
-                vmem((4, 8, LANES), F32),
+                vmem((8, 8, LANES), F32),
+                vmem((planes, devices // 8 // planes, 2, 8, LANES), F32),
+                vmem((4, 8, LANES), jnp.int32),
                 dma((11,)),
                 dma((PIECES, 2 * REACH)),
                 dma((PIECES, WINDOW)),
@@ -700,12 +738,16 @@
                 dma((2 * REACH,)),
                 dma((WINDOW,)),
                 dma((WINDOW,)),
+                dma((8,)),
+                dma((8,)),
                 dma((4,)),
                 dma((4,)),
-                dma,
-                dma,
                 dma((4,)),
                 dma((4,)),
+                dma((4,)),
+                dma((4,)),
+                dma((3,)),
+                dma((3,)),
             ],
             compiler_params=pltpu.CompilerParams(
                 collective_id=0, has_side_effects=True, vmem_limit_bytes=56 * 1024 * 1024

time: 44.4 us -> 35.8 us (0.81)
  the two profiles are of different devices: /device:TPU:1 before, /device:TPU:9 now
where the time goes in v3:
time: 35.8 us; the launch traced here: 35.6 us
  Pallas kernels  33.3 us (93%)
  local copies, waits for them, and re-layouts  1.67 us (5%)
  between operations  0.66 us (2%)
    pallas_call x1, Pallas kernels, body(): pl.pallas_call(functools.partial(kernel, devices, planes), out_shape=jax....  33.3 us
    unnamed x1, local copies, waits for them, and re-layouts  1.67 us

profile of v3, /device:TPU:9, one launch (start us, length us, event | category | flops | bytes accessed | tf_op | source)
XLA Modules:
  0.0 35.6 jit_solution(1611316891405558859)
XLA Ops:
  0.7 33.3 %shard_map.190 = f32[64,1024]{1,0:T(8,128)} custom-call(f32[64,1024]{1,0:T(8,128)} %moments.1, bf16[64,4096]{1,0:T(8,128)(2,1)} %up_0.1, bf16[16,4096]{1,0:T(8,128)(2,1)} %up_1.1, bf16[4,4096]{1,0:T(4,128)(2,1)} %up_2.1, bf16[1,4096]{1,0:T(2,128)(2,1)} %up_3.1, bf16[1792,4096]{1,0:T(8,128)(2,1)} %couple_0.1, bf16[448,4096]{1,0:T(8,128)(2,1)} %couple_1.1, ...), custom_call_target="tpu_custom_call" | custom-call | tf_op jit(solution)/shard_map/pallas_call | solution.py:699
  33.9 1.7 %copy.23 = f32[64,1024]{1,0:T(8,128)} copy(f32[64,1024]{1,0:T(8,128)} %shard_map.190) | data formatting | bytes 524288

commit v4 on v3

--- a/solution.py
+++ b/solution.py
@@ -133,7 +133,7 @@
     def exists(o):
         return jnp.logical_and(me + o >= 0, me + o < devices)
 
-    offsets = [o for o in range(-REACH, REACH + 1) if o != 0]
+    offsets = [-4, 4, -3, 3, -1, 1, -2, 2]
 
     for o in offsets:
 
@@ -179,23 +179,19 @@
     for copy in copies:
         copy.start()
 
+    natural_lane = lax.broadcasted_iota(jnp.int32, (LANES, LANES), 0)
+    wanted = (natural_lane & (RANK - 1)) * RHS + (natural_lane >> 6) * 8
+    ahead = wanted - lax.broadcasted_iota(jnp.int32, (LANES, LANES), 1)
+
     def build_perm(j, carry):
-        a = lax.broadcasted_iota(jnp.int32, (LANES, WIDTH), 0)
-        b = lax.broadcasted_iota(jnp.int32, (LANES, WIDTH), 1)
-        wanted = (a % RANK) * RHS + (a // RANK) * 8 + j
-        start = pl.multiple_of(j * LANES, LANES)
-        perm[pl.ds(start, LANES), :] = jnp.where(wanted == b, 1.0, 0.0).astype(BF16)
+        first_row = pl.multiple_of(j * LANES, LANES)
+        for n in range(WIDTH // LANES):
+            perm[pl.ds(first_row, LANES), n * LANES : (n + 1) * LANES] = jnp.where(
+                ahead == n * LANES - j, 1.0, 0.0
+            ).astype(BF16)
         return carry
 
     lax.fori_loop(0, 8, build_perm, 0)
-
-    a = lax.broadcasted_iota(jnp.int32, (512, 512), 0)
-    b = lax.broadcasted_iota(jnp.int32, (512, 512), 1)
-    by_pair[...] = jnp.where(b == (a % 32) * 16 + a // 32, 1.0, 0.0).astype(BF16)
-    a = lax.broadcasted_iota(jnp.int32, (256, 256), 0)
-    b = lax.broadcasted_iota(jnp.int32, (256, 256), 1)
-    by_row[...] = jnp.where(b == (a % 2) * 128 + a // 2, 1.0, 0.0).astype(BF16)
-
     copies[0].wait()
     own = jnp.dot(mom[...].astype(BF16), perm[...], preferred_element_type=F32).astype(BF16)
     for h in range(PIECES):
@@ -283,6 +279,13 @@
             device_id=place(to),
             device_id_type=MESH,
         )
+
+    a = lax.broadcasted_iota(jnp.int32, (512, 512), 0)
+    b = lax.broadcasted_iota(jnp.int32, (512, 512), 1)
+    by_pair[...] = jnp.where(b == (a & 31) * 16 + (a >> 5), 1.0, 0.0).astype(BF16)
+    a = lax.broadcasted_iota(jnp.int32, (256, 256), 0)
+    b = lax.broadcasted_iota(jnp.int32, (256, 256), 1)
+    by_row[...] = jnp.where(b == (a & 1) * 128 + (a >> 1), 1.0, 0.0).astype(BF16)
 
     for n in range(1, 5):
         copies[n].wait()
@@ -575,24 +578,6 @@
     start(shared)
     all_sends += shared
     far_0(1, 4, 8)
-
-    arrived_passed(win_b, recv_b)
-    copies[9].wait()
-    copies[10].wait()
-    for h in range(PIECES):
-        gathered[0:608, :] = jnp.dot(
-            hot_1[...],
-            win_b[:, :, h * PART : (h + 1) * PART].reshape(WINDOW * 32, PART),
-            preferred_element_type=F32,
-        ).astype(BF16)
-
-        def far_1(n, carry):
-            row = pl.multiple_of(n * WIDE, WIDE)
-            far_part(h, row, 1792 + row, 512 + pl.multiple_of(n * 64, 64), 7, 8)
-            return carry
-
-        lax.fori_loop(0, 2, far_1, 0)
-        far_part(h, 448, 2240, 640, 5, 5)
 
     for k in range(1, planes):
         pltpu.make_async_copy(top.at[y], top.at[y], recv_y.at[k]).wait()
@@ -639,6 +624,24 @@
             for h in range(PIECES)
         )
     )
+
+    arrived_passed(win_b, recv_b)
+    copies[9].wait()
+    copies[10].wait()
+    for h in range(PIECES):
+        gathered[0:608, :] = jnp.dot(
+            hot_1[...],
+            win_b[:, :, h * PART : (h + 1) * PART].reshape(WINDOW * 32, PART),
+            preferred_element_type=F32,
+        ).astype(BF16)
+
+        def far_1(n, carry):
+            row = pl.multiple_of(n * WIDE, WIDE)
+            far_part(h, row, 1792 + row, 512 + pl.multiple_of(n * 64, 64), 7, 8)
+            return carry
+
+        lax.fori_loop(0, 2, far_1, 0)
+        far_part(h, 448, 2240, 640, 5, 5)
 
     def lowered(parent, n, boxes):
         rows = jnp.concatenate(

time: 35.8 us -> 35.1 us (0.980)
  the two profiles are of different devices: /device:TPU:9 before, /device:TPU:1 now
where the time goes in v4:
time: 35.1 us; the launch traced here: 35 us
  Pallas kernels  32.6 us (93%)
  local copies, waits for them, and re-layouts  1.67 us (5%)
  between operations  0.66 us (2%)
    pallas_call x1, Pallas kernels, body(): pl.pallas_call(functools.partial(kernel, devices, planes), out_shape=jax....  32.6 us
    unnamed x1, local copies, waits for them, and re-layouts  1.67 us

profile of v4, /device:TPU:1, one launch (start us, length us, event | category | flops | bytes accessed | tf_op | source)
XLA Modules:
  0.0 35.0 jit_solution(13938477455556035425)
XLA Ops:
  0.7 32.6 %shard_map.190 = f32[64,1024]{1,0:T(8,128)} custom-call(f32[64,1024]{1,0:T(8,128)} %moments.1, bf16[64,4096]{1,0:T(8,128)(2,1)} %up_0.1, bf16[16,4096]{1,0:T(8,128)(2,1)} %up_1.1, bf16[4,4096]{1,0:T(4,128)(2,1)} %up_2.1, bf16[1,4096]{1,0:T(2,128)(2,1)} %up_3.1, bf16[1792,4096]{1,0:T(8,128)(2,1)} %couple_0.1, bf16[448,4096]{1,0:T(8,128)(2,1)} %couple_1.1, ...), custom_call_target="tpu_custom_call" | custom-call | tf_op jit(solution)/shard_map/pallas_call | solution.py:702
  33.3 1.7 %copy.23 = f32[64,1024]{1,0:T(8,128)} copy(f32[64,1024]{1,0:T(8,128)} %shard_map.190) | data formatting | bytes 524288

commit v5 on v4

--- a/solution.py
+++ b/solution.py
@@ -537,7 +537,7 @@
             far_part(h, row, row, pl.multiple_of(n * 64, 64), 7, 8)
             return carry
 
-        lax.fori_loop(first, last, step, 0, unroll=2)
+        lax.fori_loop(first, last, step, 0, unroll=4)
 
     arrived_direct(win_a.at[0], recv_a.at[0])
     shared = shared_rows(win_a.at[0], pass_a.at[0], recv_a.at[0])
@@ -564,15 +564,15 @@
     ]
     for copy in sends_y:
         copy.start()
+    far_0(0, 4, 8)
+
+    arrived_passed(win_a.at[1], recv_a.at[1])
+    gather_0(1)
+    far_0(1, 0, 4)
     back = member + 1 - 2 * lax.rem(member, 2)
     pltpu.make_async_copy(c4.at[back], c4.at[back], recv_c.at[0]).wait()
     sends_c.append(whole(c4.at[back], sibling, send_c.at[2], recv_c.at[2]))
     sends_c[2].start()
-    far_0(0, 4, 8)
-
-    arrived_passed(win_a.at[1], recv_a.at[1])
-    gather_0(1)
-    far_0(1, 0, 4)
     arrived_direct(win_b, recv_b)
     shared = shared_rows(win_b, pass_b, recv_b)
     start(shared)

time: 35.1 us -> 34.8 us (level)
  no operation moved by 1% of the time
where the time goes in v5:
time: 34.8 us; the launch traced here: 34.7 us
  Pallas kernels  32.3 us (93%)
  local copies, waits for them, and re-layouts  1.67 us (5%)
  between operations  0.66 us (2%)
    pallas_call x1, Pallas kernels, body(): pl.pallas_call(functools.partial(kernel, devices, planes), out_shape=jax....  32.3 us
    unnamed x1, local copies, waits for them, and re-layouts  1.67 us

profile of v5, /device:TPU:1, one launch (start us, length us, event | category | flops | bytes accessed | tf_op | source)
XLA Modules:
  0.0 34.7 jit_solution(12543785234439934709)
XLA Ops:
  0.7 32.3 %shard_map.190 = f32[64,1024]{1,0:T(8,128)} custom-call(f32[64,1024]{1,0:T(8,128)} %moments.1, bf16[64,4096]{1,0:T(8,128)(2,1)} %up_0.1, bf16[16,4096]{1,0:T(8,128)(2,1)} %up_1.1, bf16[4,4096]{1,0:T(4,128)(2,1)} %up_2.1, bf16[1,4096]{1,0:T(2,128)(2,1)} %up_3.1, bf16[1792,4096]{1,0:T(8,128)(2,1)} %couple_0.1, bf16[448,4096]{1,0:T(8,128)(2,1)} %couple_1.1, ...), custom_call_target="tpu_custom_call" | custom-call | tf_op jit(solution)/shard_map/pallas_call | solution.py:702
  33.0 1.7 %copy.23 = f32[64,1024]{1,0:T(8,128)} copy(f32[64,1024]{1,0:T(8,128)} %shard_map.190) | data formatting | bytes 524288
